TPU v7x, 512 devices: a whole 4x4x16 slice. The times are simulated.
512 devices in a mesh: member: 32 (over z, x_lo), space: 16 (over x_hi, y, core).
Axes of the slice: x: 4 (x_hi: 2, x_lo: 2; x = x_hi * 2 + x_lo), y: 4, z: 16, core: 2. Of those that a mesh axis runs over, the one named last changes fastest.
Arguments:
- perturb: bfloat16 [64, 2, 2, 1024, 3072], P('member', None, None, 'space'), may hold values from -6 to 6
- control: float32 [64, 2, 2, 128, 256], P('member', None, None, 'space'), may hold values from -6 to 6
- lat_basis: bfloat16 [1024, 128], P('space'), may hold values from -0.5 to 0.5
- lon_basis: bfloat16 [3072, 256], P('member'), may hold values from -0.375 to 0.375
- innovation: bfloat16 [2, 2, 1024, 3072], P(None, None, 'space', 'member'), may hold values from -6 to 6
- weights: bfloat16 [2, 2, 1024, 3072], P(None, None, 'space', 'member'), may hold values from 0.5 to 4
Outputs:
- increment: float32 [2, 2, 1024, 3072], P(None, None, 'space', 'member')
- gradient: float32 [64, 2, 2, 128, 256], P('member', None, None, 'space')
All inputs are finite; a program needn't handle non-finite values.
Results may differ from a plain program's by a relative error of at most 0.01.
Values may be sent and summed in bfloat16 or wider, within the bound.
No kernel may reach another device: no remote copies, remote signals or barrier semaphores. Data moves between devices by JAX's collectives and lax.ppermute only.
A program may use at most 64 MiB of HBM per device.

v0:
```python
import math

import jax
import jax.numpy as jnp
from jax import lax
from jax.sharding import PartitionSpec as P


def per_device(perturb, control, lat_basis, lon_basis, innovation, weights):
    member_count = lax.axis_size("member") * perturb.shape[0]
    factor = 1.0 / math.sqrt(member_count - 1)
    full_control = lax.all_gather(control.astype(jnp.bfloat16), "space", axis=3, tiled=True).astype(
        control.dtype
    )
    control_b = full_control.astype(jnp.bfloat16)
    lon_full = lax.all_gather(lon_basis, "member", axis=0, tiled=True)
    lat_part = jnp.einsum(
        "yk,mflkx->mflyx", lat_basis, control_b, preferred_element_type=jnp.float32
    ).astype(jnp.bfloat16)
    local_field = jnp.einsum(
        "mflyx,nx->mflyn", lat_part, lon_full, preferred_element_type=jnp.float32
    )
    partial_value = jnp.sum(perturb.astype(jnp.float32) * local_field, axis=0)
    columns = innovation.shape[3]
    summed = lax.psum(partial_value, "member") * factor
    innov_full, weights_full = (
        lax.all_gather(innovation, "member", axis=3, tiled=True),
        lax.all_gather(weights, "member", axis=3, tiled=True),
    )
    forcing = (weights_full.astype(jnp.float32) * (summed - innov_full.astype(jnp.float32))).astype(
        jnp.bfloat16
    )
    increment = lax.dynamic_slice_in_dim(summed, lax.axis_index("member") * columns, columns, 3)
    weighted = (perturb.astype(jnp.float32) * forcing.astype(jnp.float32)[None]).astype(
        jnp.bfloat16
    )
    lon_back = jnp.einsum(
        "mflyn,nx->mflyx", weighted, lon_full, preferred_element_type=jnp.float32
    ).astype(jnp.bfloat16)
    projected = jnp.einsum(
        "yk,mflyx->mflkx", lat_basis, lon_back, preferred_element_type=jnp.float32
    )
    back_rows = lax.psum_scatter(projected, "space", scatter_dimension=3, tiled=True)
    gradient = control + factor * back_rows
    return (increment, gradient)


def solution(mesh):
    return jax.shard_map(
        per_device,
        mesh=mesh,
        in_specs=(
            P("member", None, None, "space", None),
            P("member", None, None, "space", None),
            P("space", None),
            P("member", None),
            P(None, None, "space", "member"),
            P(None, None, "space", "member"),
        ),
        out_specs=(P(None, None, "space", "member"), P("member", None, None, "space", None)),
        check_vma=False,
    )
```

profile of v0, /device:TPU:1, one launch (start us, length us, event | category | flops | bytes accessed | tf_op | source)
XLA Modules:
  0.0 873.8 jit_solution(4338345929622912740)
XLA Ops:
  7.2 0.0 copy-start
  7.2 0.0 all-gather.4.cloned.1.call-start
  7.2 0.7 all-gather.4.cloned.1.call-update
  7.9 0.0 all-gather.8.cloned.1.call-start
  8.0 1.6 copy.19
  9.6 0.0 all-gather.8.cloned.1.call-update
  9.6 0.0 all-gather.6.cloned.1.call-start
  9.6 1.6 copy.17
  11.2 0.0 all-gather.6.cloned.1.call-update
  11.2 0.0 all-reduce.4.cloned.1.call-start
  11.3 0.8 convert_element_type.34
  12.1 27.5 %all_gather.12 = bf16[2,2,2,128,256]{4,3,2,1,0:T(8,128)(2,1)S(1)} all-gather(bf16[2,2,2,8,256]{4,3,2,1,0:T(8,128)(2,1)S(1)} %convert_element_type.34), channel_id=1, replica_groups=mesh['member'=32,'space'=16] {'space'}, dimensions={3}, use_global_device_ids=true | all-gather | bytes 557056 | tf_op jit(solution)/shard_map/all_gather | solution.py:12
  39.6 87.3 %all-gather.4.cloned.1.call-done = bf16[3072,256]{1,0:T(8,128)(2,1)} async-done(((bf16[96,256]{1,0:T(8,128)(2,1)}), bf16[3072,256]{1,0:T(8,128)(2,1)}) %all-gather.4.cloned.1.call-update) | async-done | bytes 1572880 | tf_op jit(solution)/shard_map/all_gather | solution.py:16
  127.0 0.0 copy-done
  127.0 5.6 fusion
  132.6 0.0 all-reduce.4.cloned.1.call-update
  132.6 0.0 all-reduce.6.cloned.1.call-start
  132.7 133.4 %all-gather.8.cloned.1.call-done = bf16[2,2,64,3072]{2,1,0,3:T(2,128)(2,1)} async-done(((bf16[2,2,64,96]{2,1,0,3:T(2,128)(2,1)}), bf16[2,2,64,3072]{2,1,0,3:T(2,128)(2,1)}) %all-gather.8.cloned.1.call-update) | async-done | bytes 1572880 | tf_op jit(solution)/shard_map/all_gather | solution.py:27
  266.1 7.4 copy.20
  273.5 129.2 %all-gather.6.cloned.1.call-done = bf16[2,2,64,3072]{2,1,0,3:T(2,128)(2,1)} async-done(((bf16[2,2,64,96]{2,1,0,3:T(2,128)(2,1)}), bf16[2,2,64,3072]{2,1,0,3:T(2,128)(2,1)}) %all-gather.6.cloned.1.call-update) | async-done | bytes 1572880 | tf_op jit(solution)/shard_map/all_gather | solution.py:28
  402.6 7.4 copy.18
  410.0 0.0 copy-start.1
  410.0 268.6 %all-reduce.4.cloned.1.call-done = f32[2,2,64,3072]{3,2,1,0:T(8,128)} async-done(((f32[2,2,64,3072]{3,2,1,0:T(8,128)}), f32[2,2,64,3072]{3,2,1,0:T(8,128)}) %all-reduce.4.cloned.1.call-update) | async-done | bytes 3145744 | tf_op jit(solution)/shard_map/psum | solution.py:25
  678.6 6.6 fusion.5
  685.2 0.0 copy-done.1
  685.2 4.8 convolution_bitcast_fusion
  690.0 0.0 copy-start.2
  690.0 2.3 copy.21
  692.3 0.0 all-reduce.6.cloned.1.call-update
  692.3 1.3 dynamic-slice
  694.2 1.7 constant_dynamic-slice_fusion
  695.9 169.8 %all-reduce.6.cloned.1.call-done = f32[2,2,2,128,256]{4,2,1,0,3:T(2,128)} async-done(((f32[2,2,2,128,256]{4,2,1,0,3:T(2,128)}), f32[2,2,2,128,256]{4,2,1,0,3:T(2,128)}) %all-reduce.6.cloned.1.call-update) | async-done | bytes 1048592
  865.7 0.0 copy-done.2
  865.7 0.9 fusion.18
  866.6 0.7 copy.23
Async XLA Ops:
  7.2 119.8 %copy-start = (bf16[64,128]{1,0:T(8,128)(2,1)S(1)}, bf16[64,128]{1,0:T(8,128)(2,1)}, u32[]{:S(2)}) copy-start(bf16[64,128]{1,0:T(8,128)(2,1)} %param.8) | copy-start | bytes 49156
  7.2 119.8 %all-gather.4.cloned.1.call-start = ((), (), s32[]{:S(2)}) async-start(), calls=%async_computation | async-start | bytes 1622016 | tf_op jit(solution)/shard_map/all_gather | solution.py:16
  7.9 258.2 %all-gather.8.cloned.1.call-start = ((), (), s32[]{:S(2)}) async-start(), calls=%async_computation.3 | async-start | bytes 3244032 | tf_op jit(solution)/shard_map/all_gather | solution.py:27
  9.6 393.0 %all-gather.6.cloned.1.call-start = ((), (), s32[]{:S(2)}) async-start(), calls=%async_computation.2 | async-start | bytes 3244032 | tf_op jit(solution)/shard_map/all_gather | solution.py:28
  11.2 667.4 %all-reduce.4.cloned.1.call-start = ((), (), s32[]{:S(2)}) async-start(), calls=%async_computation.1 | async-start | bytes 6291456 | tf_op jit(solution)/shard_map/psum | solution.py:25
  132.6 733.1 %all-reduce.6.cloned.1.call-start = ((), (), s32[]{:S(2)}) async-start(), calls=%async_computation.4 | async-start | bytes 2097152
  410.0 275.2 %copy-start.1 = (bf16[2,2,2,64,3072]{4,3,2,1,0:T(8,128)(2,1)S(1)}, bf16[2,2,2,64,3072]{4,3,2,1,0:T(8,128)(2,1)}, u32[]{:S(2)}) copy-start(bf16[2,2,2,64,3072]{4,3,2,1,0:T(8,128)(2,1)} %param.6) | copy-start | bytes 9437188
  690.0 175.7 %copy-start.2 = (f32[2,2,2,8,256]{4,3,2,1,0:T(8,128)S(1)}, f32[2,2,2,8,256]{4,3,2,1,0:T(8,128)}, u32[]{:S(2)}) copy-start(f32[2,2,2,8,256]{4,3,2,1,0:T(8,128)} %param.7) | copy-start | bytes 196612
Sparse Core Ops, SparseCore 0:
  10.1 116.8 all-gather.3
  129.6 136.4 all-gather.7
  268.2 134.4 all-gather.5
  405.4 273.1 all-reduce.3
  692.4 173.2 all-reduce.5
where the time goes:
time: 874 us
  waiting for transfers between devices  789 us (90%)
  blocking collectives  27.5 us (3%)
  local copies, waits for them, and re-layouts  23.9 us (3%)
  between operations  14.5 us (2%)
  matrix products  10.4 us (1%)
    psum x1, waiting for transfers between devices, per_device(): summed = lax.psum(partial_value, 'member') * factor  269 us
    unnamed x6, waiting for transfers between devices  171 us
    all_gather x1, waiting for transfers between devices, per_device(): lax.all_gather(innovation, 'member', axis=3, tiled=True)  133 us
    all_gather x1, waiting for transfers between devices, per_device(): lax.all_gather(weights, 'member', axis=3, tiled=True)  129 us
    all_gather x1, waiting for transfers between devices, per_device(): lon_full = lax.all_gather(lon_basis, 'member', axis=0, tiled=True)  87.3 us
    all_gather x1, blocking collectives, per_device(): lax.all_gather(control.astype(jnp.bfloat16), 'space', axis=3, tiled=True)  27.5 us
  transfers between devices with their start and end apart: 5, of which 5 were waited for; matrix products, arithmetic and copies ran while one was open for 3% of the time, Pallas kernels for 0%

commit v1 on v0

v1 whole, which is shorter than its diff:
```python
import math

import jax
import jax.numpy as jnp
from jax import lax
from jax.experimental import pallas as pl
from jax.experimental.pallas import tpu as pltpu
from jax.sharding import PartitionSpec as P

NEAR, FAR = 4, 8
ORDER = (0, 4, 2, 6, 1, 5, 3, 7)
NEAR_GROUPS = [[NEAR * far + near for near in range(NEAR)] for far in range(FAR)]
FAR_GROUPS = [[NEAR * far + near for far in ORDER] for near in range(NEAR)]
CORE_GROUPS = [[2 * chip, 2 * chip + 1] for chip in range(8)]
F32, BF16 = jnp.float32, jnp.bfloat16


def place(far):
    return (far % 2) * 4 + (far // 2 % 2) * 2 + far // 4


def spread(x, axis, groups, size):
    out = lax.all_to_all(
        jnp.broadcast_to(x[None], (size, *x.shape)), axis, 0, 0, tiled=True, axis_index_groups=groups
    )
    return out


def lon_block(lon_ref):
    return jnp.concatenate([lon_ref[half, near, 0] for near in range(NEAR) for half in range(2)], axis=0)


def forward_kernel(perturb_ref, control_ref, lat_ref, lon_ref, out_ref, part_ref):
    @pl.when(pl.program_id(0) == 0)
    def _():
        lat_part = jnp.dot(lat_ref[...], control_ref[...], preferred_element_type=F32).astype(BF16)
        for g in range(8):
            part_ref[64 * g : 64 * g + 64, :] = lat_part[:, 256 * g : 256 * g + 256]

    field = lax.dot_general(
        part_ref[...], lon_block(lon_ref), (((1,), (1,)), ((), ())), preferred_element_type=F32
    )
    terms = perturb_ref[...].astype(F32) * field
    total = (terms[:256] + terms[256:]).T.astype(BF16)
    for near in range(NEAR):
        out_ref[near, 0] = total[96 * near : 96 * near + 96]


def forcing_kernel(factor, parts_ref, innovation_ref, weights_ref, increment_ref, forcing_ref):
    summed = jnp.sum(parts_ref[...].astype(F32), axis=0) * factor
    increment = summed.T
    increment_ref[...] = increment
    forcing = weights_ref[...].astype(F32) * (increment - innovation_ref[...].astype(F32))
    forcing = forcing.T.astype(BF16)
    for far in range(FAR):
        forcing_ref[far] = forcing


def backward_kernel(perturb_ref, forcing_ref, lat_ref, lon_ref, out_ref, total_ref):
    step = pl.program_id(0)

    @pl.when(step == 0)
    def _():
        total_ref[...] = jnp.zeros_like(total_ref)

    forcing = jnp.concatenate([forcing_ref[near, 0] for near in range(NEAR)], axis=0).astype(F32).T
    weighted = perturb_ref[...].astype(F32) * jnp.concatenate([forcing, forcing], axis=0)
    total_ref[...] += jnp.dot(weighted.astype(BF16), lon_block(lon_ref), preferred_element_type=F32)

    @pl.when(step == FAR - 1)
    def _():
        lon_back = total_ref[...].astype(BF16)
        for g in range(8):
            out_ref[:, 256 * g : 256 * g + 256] = lax.dot_general(
                lat_ref[...],
                lon_back[64 * g : 64 * g + 64],
                (((0,), (0,)), ((), ())),
                preferred_element_type=F32,
            ).astype(BF16)


PERTURB_SPEC = pl.BlockSpec((512, 384), lambda far: (0, far))
LON_SPEC = pl.BlockSpec((2, NEAR, 1, 48, 256), lambda far: (0, 0, place(far), 0, 0))
GRID_SPEC = pl.BlockSpec((NEAR, 1, 96, 256), lambda far: (0, place(far), 0, 0))


def whole(*shape):
    return pl.BlockSpec(shape, lambda far: (0,) * len(shape))


def per_device(perturb, control, lat_basis, lon_basis, innovation, weights):
    factor = 1.0 / math.sqrt(63)
    params = pltpu.CompilerParams(vmem_limit_bytes=32 * 2**20)
    core = lax.axis_index("space") % 2

    lon = lax.dynamic_slice_in_dim(lon_basis, core * 48, 48, 0)
    lon = spread(lon, "member", FAR_GROUPS, FAR)
    lon = spread(lon, "member", NEAR_GROUPS, NEAR)
    lon = spread(lon, "space", CORE_GROUPS, 2)

    own = control.reshape(8, 8, 256).transpose(1, 0, 2).reshape(8, 2048)
    full_control = spread(own.astype(BF16), "space", None, 16).reshape(128, 2048)

    perturb = perturb.reshape(512, 3072)
    partial_value = pl.pallas_call(
        forward_kernel,
        grid=(FAR,),
        in_specs=[PERTURB_SPEC, whole(128, 2048), whole(64, 128), LON_SPEC],
        out_specs=GRID_SPEC,
        out_shape=jax.ShapeDtypeStruct((NEAR, FAR, 96, 256), BF16),
        scratch_shapes=[pltpu.VMEM((512, 256), BF16)],
        compiler_params=params,
    )(perturb, full_control, lat_basis, lon)
    parts = lax.all_to_all(partial_value, "member", 0, 0, tiled=True, axis_index_groups=NEAR_GROUPS)
    parts = jnp.sum(parts.astype(F32), axis=0).astype(BF16)
    parts = lax.all_to_all(parts, "member", 0, 0, tiled=True, axis_index_groups=FAR_GROUPS)
    increment, forcing = pl.pallas_call(
        lambda *refs: forcing_kernel(factor, *refs),
        out_shape=(
            jax.ShapeDtypeStruct((256, 96), F32),
            jax.ShapeDtypeStruct((FAR, 96, 256), BF16),
        ),
        compiler_params=params,
    )(parts, innovation.reshape(256, 96), weights.reshape(256, 96))
    forcing = lax.all_to_all(forcing, "member", 0, 0, tiled=True, axis_index_groups=FAR_GROUPS)
    forcing = spread(forcing, "member", NEAR_GROUPS, NEAR)

    projected = pl.pallas_call(
        backward_kernel,
        grid=(FAR,),
        in_specs=[PERTURB_SPEC, GRID_SPEC, whole(64, 128), LON_SPEC],
        out_specs=whole(128, 2048),
        out_shape=jax.ShapeDtypeStruct((128, 2048), BF16),
        scratch_shapes=[pltpu.VMEM((512, 256), F32)],
        compiler_params=params,
    )(perturb, forcing, lat_basis, lon)
    back = lax.all_to_all(projected.reshape(16, 8, 2048), "space", 0, 0, tiled=True)
    back = jnp.sum(back.astype(F32), axis=0).reshape(8, 8, 256).transpose(1, 0, 2)
    gradient = control + factor * back.reshape(control.shape)
    return (increment.reshape(innovation.shape), gradient)


def solution(mesh):
    return jax.shard_map(
        per_device,
        mesh=mesh,
        in_specs=(
            P("member", None, None, "space", None),
            P("member", None, None, "space", None),
            P("space", None),
            P("member", None),
            P(None, None, "space", "member"),
            P(None, None, "space", "member"),
        ),
        out_specs=(P(None, None, "space", "member"), P("member", None, None, "space", None)),
        check_vma=False,
    )
```

time: 874 us -> 204 us (0.23)
  waiting for transfers between devices: 789 us -> 11.4 us
  blocking collectives: 27.5 us -> 167 us
  local copies, waits for them, and re-layouts: 23.9 us -> 1.27 us
  between operations: 14.5 us -> 0.75 us
  matrix products: 10.4 us -> 0 us
  starting transfers between devices: 0.2 us -> 10.2 us
  Pallas kernels: 0 us -> 9.27 us
    all_gather x3 -> x0, waiting for transfers between devices: 350 us -> none  [the longest x1 133 us: per_device(): lax.all_gather(innovation, 'member', axis=3, tiled=True)]
    psum x1 -> x0, waiting for transfers between devices: 269 us -> none  [per_device(): summed = lax.psum(partial_value, 'member') * factor]
    unnamed x6 -> x0, waiting for transfers between devices: 171 us -> none
    all_to_all x0 -> x8, blocking collectives: none -> 167 us  [the longest x4 75.6 us: spread(): lax.all_to_all(jnp.broadcast_to(x[None], (size, *x.shape)), axis, 0, 0, t...]
    all_gather x1 -> x0, blocking collectives: 27.5 us -> none  [per_device(): lax.all_gather(control.astype(jnp.bfloat16), 'space', axis=3, tiled=True)]
    all_gather x2 -> x0, local copies, waits for them, and re-layouts: 14.8 us -> none  [the longest x1 7.4 us: per_device(): lax.all_gather(weights, 'member', axis=3, tiled=True)]
    all_to_all x0 -> x1, waiting for transfers between devices: none -> 11.4 us  [spread(): lax.all_to_all(jnp.broadcast_to(x[None], (size, *x.shape)), axis, 0, 0, t...]
    dot_general x2 -> x0, matrix products: 10.4 us -> none  [the longest x1 5.61 us: per_device(): jnp.einsum('mflyx,nx->mflyn', lat_part, lon_full, preferred_element_type=...]
  transfers between devices with their start and end apart: 5 -> 1, of which waited for: 5 -> 1; matrix products, arithmetic and copies ran while one was open for 3% -> 0% of each run, Pallas kernels for 0% -> 0%
where the time goes in v1:
time: 204 us
  blocking collectives  167 us (82%)
  waiting for transfers between devices  11.4 us (6%)
  starting transfers between devices  10.2 us (5%)
  Pallas kernels  9.27 us (5%)
  other arithmetic  3.3 us (2%)
    all_to_all x4, blocking collectives, spread(): lax.all_to_all(jnp.broadcast_to(x[None], (size, *x.shape)), axis, 0, 0, t...  75.6 us
    all_to_all x1, blocking collectives, per_device(): lax.all_to_all(forcing, 'member', 0, 0, tiled=True, axis_index_groups=FAR...  26.9 us
    all_to_all x1, blocking collectives, per_device(): lax.all_to_all(parts, 'member', 0, 0, tiled=True, axis_index_groups=FAR_G...  24.3 us
    all_to_all x1, blocking collectives, per_device(): lax.all_to_all(partial_value, 'member', 0, 0, tiled=True, axis_index_grou...  22.3 us
    all_to_all x1, blocking collectives, per_device(): lax.all_to_all(projected.reshape(16, 8, 2048), 'space', 0, 0, tiled=True)  18.1 us
    all_to_all x1, waiting for transfers between devices, spread(): lax.all_to_all(jnp.broadcast_to(x[None], (size, *x.shape)), axis, 0, 0, t...  11.4 us
    all_to_all x1, starting transfers between devices, spread(): lax.all_to_all(jnp.broadcast_to(x[None], (size, *x.shape)), axis, 0, 0, t...  10.2 us
    pallas_call x1, Pallas kernels, per_device(): pl.pallas_call(forward_kernel, grid=(FAR,), in_specs=[PERTURB_SPEC, whole...  4.38 us
  transfers between devices with their start and end apart: 1, of which 1 were waited for; matrix products, arithmetic and copies ran while one was open for 0% of the time, Pallas kernels for 0%

profile of v1, /device:TPU:1, one launch (start us, length us, event | category | flops | bytes accessed | tf_op | source)
XLA Modules:
  0.0 203.5 jit_solution(2185610477336994099)
XLA Ops:
  0.6 0.0 copy-start
  0.6 0.9 convert_element_type.21
  1.5 0.8 broadcast_in_dim.10
  2.4 10.2 %all-to-all-start = ((bf16[16,8,2048]{2,1,0:T(8,128)(2,1)}), bf16[16,8,2048]{2,1,0:T(8,128)(2,1)S(1)}, u32[]{:S(2)}, u32[]{:S(2)}) async-start(bf16[16,8,2048]{2,1,0:T(8,128)(2,1)} %broadcast_in_dim.10), calls=%async_computation | async-start | bytes 1048576 | tf_op jit(solution)/shard_map/all_to_all | solution.py:23
  12.6 0.0 copy-done
  12.6 11.4 %all-to-all-done = bf16[16,8,2048]{2,1,0:T(8,128)(2,1)S(1)} async-done(((bf16[16,8,2048]{2,1,0:T(8,128)(2,1)}), bf16[16,8,2048]{2,1,0:T(8,128)(2,1)S(1)}, u32[]{:S(2)}, u32[]{:S(2)}) %all-to-all-start) | async-done | bytes 524320 | tf_op jit(solution)/shard_map/all_to_all | solution.py:23
  24.0 24.7 %all_to_all.45 = bf16[8,48,256]{2,1,0:T(8,128)(2,1)S(1)} all-to-all(bf16[8,48,256]{2,1,0:T(8,128)(2,1)S(1)} %broadcast_in_dim.11), channel_id=1, replica_groups={{0,256,128,384,64,320,192,448},{16,272,144,400,80,336,208,464},{32,288,..., dimensions={0} | all-to-all | bytes 393216 | tf_op jit(solution)/shard_map/all_to_all | solution.py:23
  48.7 0.1 broadcast_in_dim.12
  48.8 9.8 %all_to_all.46 = bf16[4,8,48,256]{3,2,1,0:T(8,128)(2,1)S(1)} all-to-all(bf16[4,8,48,256]{3,2,1,0:T(8,128)(2,1)S(1)} %broadcast_in_dim.12), channel_id=1, replica_groups={{0,16,32,48},{64,80,96,112},{128,144,160,176},{192,208,224,240},{256,27..., dimensions={0} | all-to-all | bytes 1572864 | tf_op jit(solution)/shard_map/all_to_all | solution.py:23
  58.6 0.0 copy-start.3
  58.6 0.1 broadcast_in_dim.13
  58.7 0.0 copy-start.1
  58.7 11.6 %all_to_all.47.lon_ref = bf16[2,4,8,48,256]{4,3,2,1,0:T(8,128)(2,1)S(1)} all-to-all(bf16[2,4,8,48,256]{4,3,2,1,0:T(8,128)(2,1)S(1)} %broadcast_in_dim.13), channel_id=1, replica_groups={{0,1},{2,3},{4,5},{6,7},{8,9},{10,11},{12,13},{14,15},{16,17},{18,19},{..., dimensions={0} | all-to-all | bytes 3145728 | tf_op jit(solution)/shard_map/all_to_all | solution.py:23
  70.3 0.0 copy-done.3
  70.3 0.0 copy-done.1
  70.3 4.4 %shard_map.77 = bf16[4,8,96,256]{3,2,1,0:T(8,128)(2,1)S(1)} custom-call(bf16[512,3072]{1,0:T(8,128)(2,1)S(1)} %bitcast.16, bf16[128,2048]{1,0:T(8,128)(2,1)S(1)} %bitcast.18, bf16[64,128]{1,0:T(8,128)(2,1)S(1)} %copy-done.3, bf16[2,4,8,48,256]{4,3,2,1,0:T(8,128)(2,1)S(1)} %all_to_all.47.lon_ref), custom_call_target="tpu_custom_call" | custom-call | tf_op jit(solution)/shard_map/pallas_call | solution.py:105
  74.7 22.3 %all_to_all.48 = bf16[4,8,96,256]{3,2,1,0:T(8,128)(2,1)} all-to-all(bf16[4,8,96,256]{3,2,1,0:T(8,128)(2,1)S(1)} %shard_map.77), channel_id=1, replica_groups={{0,16,32,48},{64,80,96,112},{128,144,160,176},{192,208,224,240},{256,27..., dimensions={0} | all-to-all | bytes 3145728 | tf_op jit(solution)/shard_map/all_to_all | solution.py:114
  97.1 0.0 copy-start.4
  97.1 0.0 copy-start.5
  97.1 1.7 reduce_sum.21
  98.8 24.3 %all_to_all.49.refs_0_ = bf16[8,96,256]{2,1,0:T(8,128)(2,1)S(1)} all-to-all(bf16[8,96,256]{2,1,0:T(8,128)(2,1)S(1)} %reduce_sum.21), channel_id=1, replica_groups={{0,256,128,384,64,320,192,448},{16,272,144,400,80,336,208,464},{32,288,..., dimensions={0} | all-to-all | bytes 786432 | tf_op jit(solution)/shard_map/all_to_all | solution.py:116
  123.1 0.0 copy-done.4
  123.1 0.0 copy-done.5
  123.1 0.8 shard_map.78
  123.9 26.9 %all_to_all.50 = bf16[8,96,256]{2,1,0:T(8,128)(2,1)S(1)} all-to-all(bf16[8,96,256]{2,1,0:T(8,128)(2,1)S(1)} %get-tuple-element.5), channel_id=1, replica_groups={{0,256,128,384,64,320,192,448},{16,272,144,400,80,336,208,464},{32,288,..., dimensions={0} | all-to-all | bytes 786432 | tf_op jit(solution)/shard_map/all_to_all | solution.py:125
  150.9 0.2 broadcast_in_dim.14
  151.0 0.0 copy-start.2
  151.0 29.5 %all_to_all.51.forcing_ref = bf16[4,8,96,256]{3,2,1,0:T(8,128)(2,1)S(1)} all-to-all(bf16[4,8,96,256]{3,2,1,0:T(8,128)(2,1)S(1)} %broadcast_in_dim.14), channel_id=1, replica_groups={{0,16,32,48},{64,80,96,112},{128,144,160,176},{192,208,224,240},{256,27..., dimensions={0} | all-to-all | bytes 3145728 | tf_op jit(solution)/shard_map/all_to_all | solution.py:23
  180.5 0.0 copy-done.2
  180.5 4.1 %shard_map.79 = bf16[128,2048]{1,0:T(8,128)(2,1)S(1)} custom-call(bf16[512,3072]{1,0:T(8,128)(2,1)S(1)} %bitcast.17, bf16[4,8,96,256]{3,2,1,0:T(8,128)(2,1)S(1)} %all_to_all.51.forcing_ref, bf16[64,128]{1,0:T(8,128)(2,1)S(1)} %copy-done.3, bf16[2,4,8,48,256]{4,3,2,1,0:T(8,128)(2,1)S(1)} %all_to_all.47.lon_ref), custom_call_target="tpu_custom_call" | custom-call | tf_op jit(solution)/shard_map/pallas_call | solution.py:128
  184.6 0.0 copy-start.6
  184.6 18.1 %all_to_all.52 = bf16[16,8,2048]{2,1,0:T(8,128)(2,1)S(1)} all-to-all(bf16[16,8,2048]{2,1,0:T(8,128)(2,1)S(1)} %bitcast.19), channel_id=1, replica_groups=mesh['member'=32,'space'=16] {'space'}, dimensions={0} | all-to-all | bytes 1048576 | tf_op jit(solution)/shard_map/all_to_all | solution.py:137
  202.8 0.1 convert_reduce_fusion
  202.9 0.0 copy-done.6
  202.9 0.6 add.12
  (3 shorter events, 0.0 us)
Async XLA Ops:
  0.6 12.0 %copy-start = (bf16[96,256]{1,0:T(8,128)(2,1)S(1)}, bf16[96,256]{1,0:T(8,128)(2,1)}, u32[]{:S(2)}) copy-start(bf16[96,256]{1,0:T(8,128)(2,1)} %param.9) | copy-start | bytes 147460
  2.4 21.6 %all-to-all-start = ((bf16[16,8,2048]{2,1,0:T(8,128)(2,1)}), bf16[16,8,2048]{2,1,0:T(8,128)(2,1)S(1)}, u32[]{:S(2)}, u32[]{:S(2)}) async-start(bf16[16,8,2048]{2,1,0:T(8,128)(2,1)} %broadcast_in_dim.10), calls=%async_computation | async-start | bytes 1048576 | tf_op jit(solution)/shard_map/all_to_all | solution.py:23
  58.6 11.7 %copy-start.3 = (bf16[64,128]{1,0:T(8,128)(2,1)S(1)}, bf16[64,128]{1,0:T(8,128)(2,1)}, u32[]{:S(2)}) copy-start(bf16[64,128]{1,0:T(8,128)(2,1)} %lat_ref.3) | copy-start | bytes 49156
  58.7 11.6 %copy-start.1 = (bf16[2,2,2,64,3072]{4,3,2,1,0:T(8,128)(2,1)S(1)}, bf16[2,2,2,64,3072]{4,3,2,1,0:T(8,128)(2,1)}, u32[]{:S(2)}) copy-start(bf16[2,2,2,64,3072]{4,3,2,1,0:T(8,128)(2,1)} %param.6) | copy-start | bytes 9437188
  97.1 26.1 %copy-start.4 = (bf16[2,2,64,96]{3,2,1,0:T(8,128)(2,1)S(1)}, bf16[2,2,64,96]{3,2,1,0:T(8,128)(2,1)}, u32[]{:S(2)}) copy-start(bf16[2,2,64,96]{3,2,1,0:T(8,128)(2,1)} %param.10) | copy-start | bytes 147460
  97.1 26.1 %copy-start.5 = (bf16[2,2,64,96]{3,2,1,0:T(8,128)(2,1)S(1)}, bf16[2,2,64,96]{3,2,1,0:T(8,128)(2,1)}, u32[]{:S(2)}) copy-start(bf16[2,2,64,96]{3,2,1,0:T(8,128)(2,1)} %param.11) | copy-start | bytes 147460
  151.0 29.5 %copy-start.2 = (bf16[2,2,2,64,3072]{4,3,2,1,0:T(8,128)(2,1)S(1)}, bf16[2,2,2,64,3072]{4,3,2,1,0:T(8,128)(2,1)}, u32[]{:S(2)}) copy-start(bf16[2,2,2,64,3072]{4,3,2,1,0:T(8,128)(2,1)} %param.6) | copy-start | bytes 9437188
  184.6 18.3 %copy-start.6 = (f32[2,2,2,8,256]{4,3,2,1,0:T(8,128)S(1)}, f32[2,2,2,8,256]{4,3,2,1,0:T(8,128)}, u32[]{:S(2)}) copy-start(f32[2,2,2,8,256]{4,3,2,1,0:T(8,128)} %param.7) | copy-start | bytes 196612

commit v2 on v1

v2 whole, which is shorter than its diff:
```python
import math

import jax
import jax.numpy as jnp
from jax import lax
from jax.experimental import pallas as pl
from jax.experimental.pallas import tpu as pltpu
from jax.sharding import Mesh, PartitionSpec as P

PAIR, RING, NEAR, FAR, PLANE = 2, 16, 2, 8, 32
ORDER = (0, 4, 2, 6, 1, 5, 3, 7)
NEAR_GROUPS = [[NEAR * far + near for near in range(NEAR)] for far in range(FAR)]
FAR_GROUPS = [[NEAR * far + near for far in ORDER] for near in range(NEAR)]
F32, BF16 = jnp.float32, jnp.bfloat16


def place(far):
    return (far % 2) * 4 + (far // 2 % 2) * 2 + far // 4


def columns_kernel(perturb_ref, control_ref, lon_ref, *refs):
    outs, (own_ref, copy_ref, turned_ref) = refs[:PAIR], refs[PAIR:]

    @pl.when(pl.program_id(0) == 0)
    def _():
        copy_ref[...] = lon_ref[...]
        for g in range(8):
            own = control_ref[8 * g : 8 * g + 8, :]
            own = jnp.concatenate([own, own], axis=0).astype(BF16)
            for pair in range(PLANE // 2):
                own_ref[16 * pair : 16 * pair + 16, 256 * g : 256 * g + 256] = own

    turned_ref[...] = perturb_ref[...].astype(F32).T.astype(BF16)
    me = lax.axis_index("pair")
    for other in range(PAIR):
        for z in range(2):
            start = pl.multiple_of(192 * z + 96 * (me ^ other), 96)
            outs[other][96 * z : 96 * z + 96, :] = turned_ref[pl.ds(start, 96), :]


def forward_kernel(own_ref, traded_ref, control_ref, lat_ref, lon_ref, out_ref, part_ref):
    @pl.when(pl.program_id(0) == 0)
    def _():
        for pair in range(PAIR):
            control = control_ref[128 * pair : 128 * pair + 128, :]
            lat_part = jnp.dot(lat_ref[...], control, preferred_element_type=F32).astype(BF16)
            for g in range(8):
                part_ref[pair, 64 * g : 64 * g + 64, :] = lat_part[:, 256 * g : 256 * g + 256]

    me = lax.axis_index("pair")
    total = jnp.zeros((192, 256), F32)
    for other, perturb_ref in enumerate((own_ref, traded_ref)):
        field = lax.dot_general(
            lon_ref[...], part_ref[me ^ other], (((1,), (1,)), ((), ())), preferred_element_type=F32
        )
        terms = perturb_ref[...].astype(F32) * field
        total += terms[:, :256] + terms[:, 256:]
    total = total.astype(BF16)
    for near in range(NEAR):
        out_ref[near, 0] = total[96 * near : 96 * near + 96]


def forcing_kernel(factor, parts_ref, innovation_ref, weights_ref, increment_ref, forcing_ref):
    summed = jnp.sum(parts_ref[...].astype(F32), axis=0) * factor
    increment = summed.T
    increment_ref[...] = increment
    forcing = weights_ref[...].astype(F32) * (increment - innovation_ref[...].astype(F32))
    forcing_ref[...] = forcing.T.astype(BF16)


def backward_kernel(own_ref, traded_ref, forcing_ref, lat_ref, lon_ref, out_ref, total_ref):
    step = pl.program_id(0)

    @pl.when(step == 0)
    def _():
        total_ref[...] = jnp.zeros_like(total_ref)

    forcing = forcing_ref[...].astype(F32)
    forcing = jnp.concatenate([forcing, forcing], axis=1)
    for other, perturb_ref in enumerate((own_ref, traded_ref)):
        weighted = (perturb_ref[...].astype(F32) * forcing).astype(BF16)
        total_ref[other] += lax.dot_general(
            weighted, lon_ref[...], (((0,), (0,)), ((), ())), preferred_element_type=F32
        )

    @pl.when(step == pl.num_programs(0) - 1)
    def _():
        me = lax.axis_index("pair")
        for other in range(PAIR):
            lon_back = total_ref[other].astype(BF16)
            for g in range(8):
                out_ref[me ^ other, :, 256 * g : 256 * g + 256] = lax.dot_general(
                    lat_ref[...],
                    lon_back[64 * g : 64 * g + 64],
                    (((0,), (0,)), ((), ())),
                    preferred_element_type=F32,
                ).astype(BF16)


def whole(*shape):
    return pl.BlockSpec(shape, lambda step: (0,) * len(shape))


def rows_of(rows, width):
    return pl.BlockSpec((rows, width), lambda step: (step, 0))


def shape_of(shape, dtype=BF16):
    return jax.ShapeDtypeStruct(shape, dtype)


def per_device(perturb, control, lat_basis, lon_basis, innovation, weights):
    factor = 1.0 / math.sqrt(63)
    params = pltpu.CompilerParams(vmem_limit_bytes=40 * 2**20)

    own, other, own_control, lon = pl.pallas_call(
        columns_kernel,
        grid=(8,),
        in_specs=[pl.BlockSpec((512, 384), lambda step: (0, step)), whole(64, 256), whole(96, 256)],
        out_specs=[rows_of(192, 512)] * PAIR + [whole(8 * PLANE, 2048), whole(96, 256)],
        out_shape=[shape_of((1536, 512))] * PAIR + [shape_of((8 * PLANE, 2048)), shape_of((96, 256))],
        scratch_shapes=[pltpu.VMEM((384, 512), BF16)],
        compiler_params=params,
    )(perturb.reshape(512, 3072), control.reshape(64, 256), lon_basis)
    traded = lax.ppermute(other, "pair", [(0, 1), (1, 0)])
    full_control = lax.all_to_all(own_control, ("pair", "space"), 0, 0, tiled=True)
    lon = lax.all_gather(lon, "z", axis=0, tiled=True)

    parts = pl.pallas_call(
        forward_kernel,
        grid=(8,),
        in_specs=[rows_of(192, 512)] * PAIR + [whole(256, 2048), whole(64, 128), rows_of(192, 256)],
        out_specs=pl.BlockSpec((NEAR, 1, 96, 256), lambda step: (0, place(step), 0, 0)),
        out_shape=shape_of((NEAR, FAR, 96, 256)),
        scratch_shapes=[pltpu.VMEM((PAIR, 512, 256), BF16)],
        compiler_params=params,
    )(own, traded, full_control, lat_basis, lon)
    parts = lax.all_to_all(parts, "z", 0, 0, tiled=True, axis_index_groups=NEAR_GROUPS)
    parts = jnp.sum(parts.astype(F32), axis=0).astype(BF16)
    parts = lax.all_to_all(parts, "z", 0, 0, tiled=True, axis_index_groups=FAR_GROUPS)
    increment, forcing = pl.pallas_call(
        lambda *refs: forcing_kernel(factor, *refs),
        out_shape=(shape_of((256, 96), F32), shape_of((96, 256))),
        compiler_params=params,
    )(parts, innovation.reshape(256, 96), weights.reshape(256, 96))
    forcing = lax.all_gather(forcing, "z", axis=0, tiled=True)

    projected = pl.pallas_call(
        backward_kernel,
        grid=(6,),
        in_specs=[rows_of(256, 512)] * PAIR + [rows_of(256, 256), whole(64, 128), rows_of(256, 256)],
        out_specs=whole(PAIR, 128, 2048),
        out_shape=shape_of((PAIR, 128, 2048)),
        scratch_shapes=[pltpu.VMEM((PAIR, 512, 256), F32)],
        compiler_params=params,
    )(own, traded, forcing, lat_basis, lon)
    back = lax.all_to_all(projected.reshape(8 * PLANE, 2048), ("pair", "space"), 0, 0, tiled=True)
    back = jnp.sum(back.astype(F32).reshape(PLANE, 8, 2048), axis=0)
    back = back.reshape(8, 8, 256).transpose(1, 0, 2)
    gradient = control + factor * back.reshape(control.shape)
    return (increment.reshape(innovation.shape), gradient)


def solution(mesh):
    members = ("z", "pair")
    devices = mesh.devices.reshape(RING, PAIR, mesh.shape["space"])
    return jax.shard_map(
        per_device,
        mesh=Mesh(devices, (*members, "space")),
        in_specs=(
            P(members, None, None, "space", None),
            P(members, None, None, "space", None),
            P("space", None),
            P(members, None),
            P(None, None, "space", members),
            P(None, None, "space", members),
        ),
        out_specs=(P(None, None, "space", members), P(members, None, None, "space", None)),
        check_vma=False,
    )
```

time: 204 us -> 185 us (0.907)
  blocking collectives: 167 us -> 139 us
  Pallas kernels: 9.27 us -> 16 us
  local copies, waits for them, and re-layouts: 1.27 us -> 4.53 us
  starting transfers between devices: 10.2 us -> 12.5 us
    all_to_all x8 -> x3, blocking collectives: 167 us -> 79.3 us  [the longest x1 36.5 us: per_device(): lax.all_to_all(parts, 'z', 0, 0, tiled=True, axis_index_groups=FAR_GROUPS)]
    all_gather x0 -> x2, blocking collectives: none -> 60.1 us  [the longest x1 32.9 us: per_device(): lon = lax.all_gather(lon, 'z', axis=0, tiled=True)]
    pallas_call x3 -> x4, Pallas kernels: 9.27 us -> 16 us  [the longest x1 6.02 us: per_device(): pl.pallas_call(forward_kernel, grid=(8,), in_specs=[rows_of(192, 512)] *...]
    unnamed x14 -> x16, local copies, waits for them, and re-layouts: 0.04 us -> 4.53 us
    ppermute x0 -> x1, starting transfers between devices: none -> 4.06 us  [per_device(): traded = lax.ppermute(other, 'pair', [(0, 1), (1, 0)])]
  transfers between devices with their start and end apart: 1 -> 2, of which waited for: 1 -> 1; matrix products, arithmetic and copies ran while one was open for 0% -> 0% of each run, Pallas kernels for 0% -> 0%
where the time goes in v2:
time: 185 us; the launch traced here: 184 us
  blocking collectives  139 us (75%)
  Pallas kernels  16 us (9%)
  starting transfers between devices  12.5 us (7%)
  waiting for transfers between devices  9.44 us (5%)
  local copies, waits for them, and re-layouts  4.53 us (2%)
    all_to_all x1, blocking collectives, per_device(): lax.all_to_all(parts, 'z', 0, 0, tiled=True, axis_index_groups=FAR_GROUPS)  36.5 us
    all_gather x1, blocking collectives, per_device(): lon = lax.all_gather(lon, 'z', axis=0, tiled=True)  32.9 us
    all_to_all x1, blocking collectives, per_device(): lax.all_to_all(projected.reshape(8 * PLANE, 2048), ('pair', 'space'), 0,...  29 us
    all_gather x1, blocking collectives, per_device(): forcing = lax.all_gather(forcing, 'z', axis=0, tiled=True)  27.2 us
    all_to_all x1, blocking collectives, per_device(): lax.all_to_all(parts, 'z', 0, 0, tiled=True, axis_index_groups=NEAR_GROUPS)  13.7 us
    all_to_all x1, waiting for transfers between devices, per_device(): lax.all_to_all(own_control, ('pair', 'space'), 0, 0, tiled=True)  9.43 us
    all_to_all x1, starting transfers between devices, per_device(): lax.all_to_all(own_control, ('pair', 'space'), 0, 0, tiled=True)  8.46 us
    pallas_call x1, Pallas kernels, per_device(): pl.pallas_call(forward_kernel, grid=(8,), in_specs=[rows_of(192, 512)] *...  6.02 us
  transfers between devices with their start and end apart: 2, of which 1 were waited for; matrix products, arithmetic and copies ran while one was open for 0% of the time, Pallas kernels for 0%

profile of v2, /device:TPU:1, one launch (start us, length us, event | category | flops | bytes accessed | tf_op | source)
XLA Modules:
  0.0 184.3 jit_solution(5135709155175249144)
XLA Ops:
  0.6 0.0 copy-start
  0.6 1.9 %copy-done = bf16[2,2,2,64,3072]{4,3,2,1,0:T(8,128)(2,1)S(1)} copy-done((bf16[2,2,2,64,3072]{4,3,2,1,0:T(8,128)(2,1)S(1)}, bf16[2,2,2,64,3072]{4,3,2,1,0:T(8,128)(2,1)}, u32[]{:S(2)}) %copy-start) | copy-done | bytes 3145752
  2.5 0.0 copy-start.2
  2.5 0.8 copy-done.2
  3.4 0.0 copy-start.7
  3.4 0.8 copy-done.7
  4.2 4.3 %shard_map.77 = (bf16[1536,512]{1,0:T(8,128)(2,1)S(1)}, bf16[1536,512]{1,0:T(8,128)(2,1)}, bf16[256,2048]{1,0:T(8,128)(2,1)S(1)}, bf16[96,256]{1,0:T(8,128)(2,1)S(1)}) custom-call(bf16[512,3072]{1,0:T(8,128)(2,1)S(1)} %bitcast.15, f32[64,256]{1,0:T(8,128)S(1)} %bitcast.17, bf16[96,256]{1,0:T(8,128)(2,1)S(1)} %copy-done.7), custom_call_target="tpu_custom_call" | custom-call | tf_op jit(solution)/shard_map/pallas_call | solution.py:116
  8.4 0.0 copy-start.1
  8.4 1.0 copy-done.1
  9.4 0.0 copy-start.4
  9.4 4.1 %collective-permute-start = (bf16[1536,512]{1,0:T(8,128)(2,1)}, bf16[1536,512]{1,0:T(8,128)(2,1)}, u32[]{:S(2)}, u32[]{:S(2)}) collective-permute-start(bf16[1536,512]{1,0:T(8,128)(2,1)} %get-tuple-element.9), channel_id=1, source_target_pairs={{0,16},{16,0},{1,17},{17,1},{2,18},{18,2},{3,19},{19,3},{4,20},{20... | collective-permute-start | bytes 4718600 | tf_op jit(solution)/shard_map/ppermute | solution.py:125
  13.5 8.5 %all-to-all-start = ((bf16[32,8,2048]{2,1,0:T(8,128)(2,1)}), bf16[32,8,2048]{2,1,0:T(8,128)(2,1)S(1)}, u32[]{:S(2)}, u32[]{:S(2)}) async-start(bf16[32,8,2048]{2,1,0:T(8,128)(2,1)} %bitcast.16), calls=%async_computation | async-start | bytes 2097152 | tf_op jit(solution)/shard_map/all_to_all | solution.py:126
  21.9 32.9 %all_gather.6.lon_ref = bf16[1536,256]{1,0:T(8,128)(2,1)S(1)} all-gather(bf16[96,256]{1,0:T(8,128)(2,1)S(1)} %get-tuple-element.11), channel_id=1, replica_groups=mesh['z'=16,'pair'=2,'space'=16] {'z'}, dimensions={0}, use_global_device_ids=true | all-gather | bytes 835584 | tf_op jit(solution)/shard_map/all_gather | solution.py:127
  54.9 9.4 %all-to-all-done = bf16[32,8,2048]{2,1,0:T(8,128)(2,1)S(1)} async-done(((bf16[32,8,2048]{2,1,0:T(8,128)(2,1)}), bf16[32,8,2048]{2,1,0:T(8,128)(2,1)S(1)}, u32[]{:S(2)}, u32[]{:S(2)}) %all-to-all-start) | async-done | bytes 1048608 | tf_op jit(solution)/shard_map/all_to_all | solution.py:126
  64.3 0.0 collective-permute-done.traded_ref
  64.3 0.0 copy-done.4
  64.3 6.0 %shard_map.78 = bf16[2,8,96,256]{3,2,1,0:T(8,128)(2,1)S(1)} custom-call(bf16[1536,512]{1,0:T(8,128)(2,1)S(1)} %get-tuple-element.8.own_ref, bf16[1536,512]{1,0:T(8,128)(2,1)} %collective-permute-done.traded_ref, bf16[256,2048]{1,0:T(8,128)(2,1)S(1)} %bitcast.13, bf16[64,128]{1,0:T(8,128)(2,1)S(1)} %copy-done.4, bf16[1536,256]{1,0:T(8,128)(2,1)S(1)} %all_gather.6.lon_ref), custom_call_target="tpu_custom_call" | custom-call | tf_op jit(solution)/shard_map/pallas_call | solution.py:129
  70.3 0.0 copy-start.5
  70.3 0.0 copy-start.6
  70.4 13.7 %all_to_all.30 = bf16[2,8,96,256]{3,2,1,0:T(8,128)(2,1)S(1)} all-to-all(bf16[2,8,96,256]{3,2,1,0:T(8,128)(2,1)S(1)} %shard_map.78), channel_id=1, replica_groups={{0,32},{64,96},{128,160},{192,224},{256,288},{320,352},{384,416},{448,4..., dimensions={0} | all-to-all | bytes 1572864 | tf_op jit(solution)/shard_map/all_to_all | solution.py:138
  84.1 1.0 reduce_sum.21
  85.1 36.5 %all_to_all.31.refs_0_ = bf16[8,96,256]{2,1,0:T(8,128)(2,1)S(1)} all-to-all(bf16[8,96,256]{2,1,0:T(8,128)(2,1)} %reduce_sum.21), channel_id=1, replica_groups={{0,256,128,384,64,320,192,448},{32,288,160,416,96,352,224,480},{1,257,1..., dimensions={0} | all-to-all | bytes 786432 | tf_op jit(solution)/shard_map/all_to_all | solution.py:140
  121.6 0.0 copy-done.5
  121.6 0.0 copy-done.6
  121.6 0.8 shard_map.79
  122.4 27.2 %all_gather.7.forcing_ref = bf16[1536,256]{1,0:T(8,128)(2,1)S(1)} all-gather(bf16[96,256]{1,0:T(8,128)(2,1)S(1)} %get-tuple-element.13), channel_id=1, replica_groups=mesh['z'=16,'pair'=2,'space'=16] {'z'}, dimensions={0}, use_global_device_ids=true | all-gather | bytes 835584 | tf_op jit(solution)/shard_map/all_gather | solution.py:146
  149.6 4.9 %shard_map.80 = bf16[2,128,2048]{2,1,0:T(8,128)(2,1)S(1)} custom-call(bf16[1536,512]{1,0:T(8,128)(2,1)S(1)} %get-tuple-element.8.own_ref, bf16[1536,512]{1,0:T(8,128)(2,1)} %collective-permute-done.traded_ref, bf16[1536,256]{1,0:T(8,128)(2,1)S(1)} %all_gather.7.forcing_ref, bf16[64,128]{1,0:T(8,128)(2,1)S(1)} %copy-done.4, ...), custom_call_target="tpu_custom_call" | custom-call | tf_op jit(solution)/shard_map/pallas_call | solution.py:148
  154.5 0.0 copy-start.3
  154.5 29.0 %all_to_all.32 = bf16[32,8,2048]{2,1,0:T(8,128)(2,1)S(1)} all-to-all(bf16[32,8,2048]{2,1,0:T(8,128)(2,1)S(1)} %bitcast.14), channel_id=1, replica_groups=mesh['z'=16,'pair'=2,'space'=16] {'pair','space'}, dimensions={0} | all-to-all | bytes 2097152 | tf_op jit(solution)/shard_map/all_to_all | solution.py:157
  183.5 0.2 convert_reduce_fusion
  183.7 0.0 copy-done.3
  183.7 0.6 add.3
  (1 shorter events, 0.0 us)
Async XLA Ops:
  0.6 1.9 %copy-start = (bf16[2,2,2,64,3072]{4,3,2,1,0:T(8,128)(2,1)S(1)}, bf16[2,2,2,64,3072]{4,3,2,1,0:T(8,128)(2,1)}, u32[]{:S(2)}) copy-start(bf16[2,2,2,64,3072]{4,3,2,1,0:T(8,128)(2,1)} %param.6) | copy-start | bytes 9437188
  2.5 0.8 copy-start.2
  3.4 0.8 copy-start.7
  8.4 1.0 copy-start.1
  9.4 54.9 %copy-start.4 = (bf16[64,128]{1,0:T(8,128)(2,1)S(1)}, bf16[64,128]{1,0:T(8,128)(2,1)}, u32[]{:S(2)}) copy-start(bf16[64,128]{1,0:T(8,128)(2,1)} %lat_ref.3) | copy-start | bytes 49156
  9.4 54.9 %collective-permute-start = (bf16[1536,512]{1,0:T(8,128)(2,1)}, bf16[1536,512]{1,0:T(8,128)(2,1)}, u32[]{:S(2)}, u32[]{:S(2)}) collective-permute-start(bf16[1536,512]{1,0:T(8,128)(2,1)} %get-tuple-element.9), channel_id=1, source_target_pairs={{0,16},{16,0},{1,17},{17,1},{2,18},{18,2},{3,19},{19,3},{4,20},{20... | collective-permute-start | bytes 4718600 | tf_op jit(solution)/shard_map/ppermute | solution.py:125
  13.5 50.8 %all-to-all-start = ((bf16[32,8,2048]{2,1,0:T(8,128)(2,1)}), bf16[32,8,2048]{2,1,0:T(8,128)(2,1)S(1)}, u32[]{:S(2)}, u32[]{:S(2)}) async-start(bf16[32,8,2048]{2,1,0:T(8,128)(2,1)} %bitcast.16), calls=%async_computation | async-start | bytes 2097152 | tf_op jit(solution)/shard_map/all_to_all | solution.py:126
  70.3 51.3 %copy-start.5 = (bf16[2,2,64,96]{3,2,1,0:T(8,128)(2,1)S(1)}, bf16[2,2,64,96]{3,2,1,0:T(8,128)(2,1)}, u32[]{:S(2)}) copy-start(bf16[2,2,64,96]{3,2,1,0:T(8,128)(2,1)} %param.10) | copy-start | bytes 147460
  70.3 51.3 %copy-start.6 = (bf16[2,2,64,96]{3,2,1,0:T(8,128)(2,1)S(1)}, bf16[2,2,64,96]{3,2,1,0:T(8,128)(2,1)}, u32[]{:S(2)}) copy-start(bf16[2,2,64,96]{3,2,1,0:T(8,128)(2,1)} %param.11) | copy-start | bytes 147460
  154.5 29.2 %copy-start.3 = (f32[2,2,2,8,256]{4,3,2,1,0:T(8,128)S(1)}, f32[2,2,2,8,256]{4,3,2,1,0:T(8,128)}, u32[]{:S(2)}) copy-start(f32[2,2,2,8,256]{4,3,2,1,0:T(8,128)} %param.7) | copy-start | bytes 196612

commit v3 on v2

v3 whole, which is shorter than its diff:
```python
import math

import jax
import jax.numpy as jnp
from jax import lax
from jax.experimental import pallas as pl
from jax.experimental.pallas import tpu as pltpu
from jax.sharding import Mesh, PartitionSpec as P

PAIR, RING, CHIPS, CORES, NEAR, FAR = 2, 16, 8, 2, 2, 8
ORDER = (0, 4, 2, 6, 1, 5, 3, 7)
NEAR_GROUPS = [[NEAR * far + near for near in range(NEAR)] for far in range(FAR)]
FAR_GROUPS = [[NEAR * far + near for far in ORDER] for near in range(NEAR)]
SWAP = [(0, 1), (1, 0)]
F32, BF16 = jnp.float32, jnp.bfloat16


def place(far):
    return ((far & 1) << 2) | (far & 2) | (far >> 2)


def half_basis(lat_ref, core):
    held = lax.broadcasted_iota(jnp.int32, (128, 64), 0)
    wanted = lax.broadcasted_iota(jnp.int32, (128, 64), 1)
    wanted = ((wanted >> 3) << 4) + (wanted & 7) + 8 * core
    pick = jnp.where(held == wanted, 1.0, 0.0).astype(BF16)
    return jnp.dot(lat_ref[...], pick, preferred_element_type=F32).astype(BF16)


def columns_kernel(perturb_ref, lon_ref, *refs):
    outs, (copy_ref, turned_ref) = refs[:PAIR], refs[PAIR:]
    copy_ref[...] = lon_ref[...]
    turned_ref[...] = perturb_ref[...].astype(F32).T.astype(BF16)
    me = lax.axis_index("pair")
    for other in range(PAIR):
        for z in range(RING):
            start = pl.multiple_of(192 * z + 96 * (me ^ other), 96)
            outs[other][0, 96 * z : 96 * z + 96, :] = turned_ref[pl.ds(start, 96), :]


def forward_kernel(own_ref, traded_ref, control_ref, lat_ref, lon_ref, out_ref, part_ref):
    step = pl.program_id(0)

    @pl.when(step == 0)
    def _():
        for pair in range(PAIR):
            control = control_ref[128 * pair : 128 * pair + 128, :]
            lat_part = jnp.dot(lat_ref[...], control, preferred_element_type=F32).astype(BF16)
            for g in range(8):
                part_ref[pair, 64 * g : 64 * g + 64, :] = lat_part[:, 256 * g : 256 * g + 256]

    me = lax.axis_index("pair")
    halves = [jnp.zeros((384, 128), F32), jnp.zeros((384, 128), F32)]
    for other, perturb_ref in enumerate((own_ref, traded_ref)):
        field = lax.dot_general(
            lon_ref[...], part_ref[me ^ other], (((1,), (1,)), ((), ())), preferred_element_type=F32
        )
        for block in range(4):
            halves[block % 2] += perturb_ref[block].astype(F32) * field[:, 128 * block : 128 * block + 128]
    for half in range(2):
        total = halves[half].astype(BF16)
        for z in range(4):
            far = 2 * step + z // 2
            out_ref[z % 2, place(far), :, 128 * half : 128 * half + 128] = total[96 * z : 96 * z + 96]


def forcing_kernel(factor, parts_ref, innovation_ref, weights_ref, increment_ref, forcing_ref):
    summed = jnp.sum(parts_ref[...].astype(F32), axis=0) * factor
    increment = summed.T
    increment_ref[...] = increment
    forcing = weights_ref[...].astype(F32) * (increment - innovation_ref[...].astype(F32))
    forcing_ref[...] = forcing.T.astype(BF16)


def backward_kernel(own_ref, traded_ref, forcing_ref, lat_ref, lon_ref, keep_ref, give_ref, total_ref):
    step = pl.program_id(0)

    @pl.when(step == 0)
    def _():
        total_ref[...] = jnp.zeros_like(total_ref)

    forcing = forcing_ref[...].astype(F32)
    for other, perturb_ref in enumerate((own_ref, traded_ref)):
        for block in range(4):
            half = 128 * (block % 2)
            weighted = (perturb_ref[block].astype(F32) * forcing[:, half : half + 128]).astype(BF16)
            total_ref[other, 128 * block : 128 * block + 128, :] += lax.dot_general(
                weighted, lon_ref[...], (((0,), (0,)), ((), ())), preferred_element_type=F32
            )

    @pl.when(step == pl.num_programs(0) - 1)
    def _():
        me, core = lax.axis_index("pair"), lax.axis_index("core")
        lat_mine, lat_swapped = half_basis(lat_ref, core), half_basis(lat_ref, 1 - core)
        for other in range(PAIR):
            rows = pl.ds(pl.multiple_of(64 * (me ^ other), 64), 64)
            lon_back = total_ref[other].astype(BF16)
            for g in range(8):
                part = lon_back[64 * g : 64 * g + 64]
                for lat, out_ref in ((lat_mine, keep_ref), (lat_swapped, give_ref)):
                    out_ref[rows, 256 * g : 256 * g + 256] = lax.dot_general(
                        lat, part, (((0,), (0,)), ((), ())), preferred_element_type=F32
                    ).astype(out_ref.dtype)


def add_kernel(keep_ref, got_ref, out_ref):
    out_ref[...] = (keep_ref[...] + got_ref[...].astype(F32)).astype(BF16)


def whole(*shape):
    return pl.BlockSpec(shape, lambda step: (0,) * len(shape))


def rows_of(*shape):
    return pl.BlockSpec(shape, lambda step: (0,) * (len(shape) - 2) + (step, 0))


def shape_of(shape, dtype=BF16):
    return jax.ShapeDtypeStruct(shape, dtype)


def per_device(perturb, control, lat_basis, lon_basis, innovation, weights):
    factor = 1.0 / math.sqrt(63)
    params = pltpu.CompilerParams(vmem_limit_bytes=40 * 2**20)

    own_control = control.reshape(8, 8, 256).transpose(1, 0, 2).reshape(8, 2048).astype(BF16)
    own_control = jnp.broadcast_to(own_control, (PAIR * CHIPS * CORES, 8, 2048)).reshape(256, 2048)
    own, other, lon = pl.pallas_call(
        columns_kernel,
        grid=(4,),
        in_specs=[rows_of(128, 3072), whole(96, 256)],
        out_specs=[pl.BlockSpec((1, 1536, 128), lambda step: (step, 0, 0))] * PAIR + [whole(96, 256)],
        out_shape=[shape_of((4, 1536, 128))] * PAIR + [shape_of((96, 256))],
        scratch_shapes=[pltpu.VMEM((3072, 128), BF16)],
        compiler_params=pltpu.CompilerParams(vmem_limit_bytes=60 * 2**20),
    )(perturb.reshape(512, 3072), lon_basis)
    traded = lax.ppermute(other, "pair", SWAP)
    lon = lax.all_gather(lon, "z", axis=0, tiled=True)
    full_control = lax.all_to_all(own_control, ("pair", "chip", "core"), 0, 0, tiled=True)

    parts = pl.pallas_call(
        forward_kernel,
        grid=(4,),
        in_specs=[rows_of(4, 384, 128)] * PAIR
        + [whole(256, 2048), whole(64, 128), rows_of(384, 256)],
        out_specs=whole(NEAR, FAR, 96, 256),
        out_shape=shape_of((NEAR, FAR, 96, 256)),
        scratch_shapes=[pltpu.VMEM((PAIR, 512, 256), BF16)],
        compiler_params=params,
    )(own, traded, full_control, lat_basis, lon)
    parts = lax.all_to_all(parts, "z", 0, 0, tiled=True, axis_index_groups=NEAR_GROUPS)
    parts = jnp.sum(parts.astype(F32), axis=0).astype(BF16)
    parts = lax.all_to_all(parts, "z", 0, 0, tiled=True, axis_index_groups=FAR_GROUPS)
    increment, forcing = pl.pallas_call(
        lambda *refs: forcing_kernel(factor, *refs),
        out_shape=(shape_of((256, 96), F32), shape_of((96, 256))),
        compiler_params=params,
    )(parts, innovation.reshape(256, 96), weights.reshape(256, 96))
    forcing = lax.all_gather(forcing, "z", axis=0, tiled=True)

    keep, give = pl.pallas_call(
        backward_kernel,
        grid=(3,),
        in_specs=[rows_of(4, 512, 128)] * PAIR + [rows_of(512, 256), whole(64, 128), rows_of(512, 256)],
        out_specs=[whole(128, 2048)] * 2,
        out_shape=[shape_of((128, 2048), F32), shape_of((128, 2048))],
        scratch_shapes=[pltpu.VMEM((PAIR, 512, 256), F32)],
        compiler_params=params,
    )(own, traded, forcing, lat_basis, lon)
    got = lax.ppermute(give, "core", SWAP)
    back = pl.pallas_call(add_kernel, out_shape=shape_of((128, 2048)), compiler_params=params)(keep, got)
    back = lax.all_to_all(back, ("pair", "chip"), 0, 0, tiled=True)
    back = jnp.sum(back.astype(F32).reshape(PAIR * CHIPS, 8, 2048), axis=0)
    back = back.reshape(8, 8, 256).transpose(1, 0, 2)
    gradient = control + factor * back.reshape(control.shape)
    return (increment.reshape(innovation.shape), gradient)


def solution(mesh):
    members, space = ("z", "pair"), ("chip", "core")
    devices = mesh.devices.reshape(RING, PAIR, CHIPS, CORES)
    return jax.shard_map(
        per_device,
        mesh=Mesh(devices, (*members, *space)),
        in_specs=(
            P(members, None, None, space, None),
            P(members, None, None, space, None),
            P(space, None),
            P(members, None),
            P(None, None, space, members),
            P(None, None, space, members),
        ),
        out_specs=(P(None, None, space, members), P(members, None, None, space, None)),
        check_vma=False,
    )
```

time: 185 us -> 174 us (0.941)
  blocking collectives: 139 us -> 124 us
  starting transfers between devices: 12.5 us -> 23.3 us
  local copies, waits for them, and re-layouts: 4.53 us -> 1.16 us
  Pallas kernels: 16 us -> 13.3 us
    all_to_all x1, blocking collectives: 29 us -> 12.8 us  [per_device(): back = lax.all_to_all(back, ('pair', 'chip'), 0, 0, tiled=True)]
    ppermute x1 -> x2, starting transfers between devices: 4.06 us -> 14.8 us  [the longest x1 10.8 us: per_device(): got = lax.ppermute(give, 'core', SWAP)]
    unnamed x16 -> x12, local copies, waits for them, and re-layouts: 4.53 us -> 0.03 us
    pallas_call x3 -> x4, Pallas kernels: 15.2 us -> 12.5 us  [the longest x1 4.88 us: per_device(): pl.pallas_call(columns_kernel, grid=(4,), in_specs=[rows_of(128, 3072), w...]
  transfers between devices with their start and end apart: 2 -> 3, of which waited for: 1 -> 2; matrix products, arithmetic and copies ran while one was open for 0% -> 1% of each run, Pallas kernels for 0% -> 0%
where the time goes in v3:
time: 174 us; the launch traced here: 173 us
  blocking collectives  124 us (71%)
  starting transfers between devices  23.3 us (13%)
  Pallas kernels  13.3 us (8%)
  waiting for transfers between devices  9.35 us (5%)
    all_to_all x1, blocking collectives, per_device(): lax.all_to_all(parts, 'z', 0, 0, tiled=True, axis_index_groups=FAR_GROUPS)  36.5 us
    all_gather x1, blocking collectives, per_device(): lon = lax.all_gather(lon, 'z', axis=0, tiled=True)  33.3 us
    all_gather x1, blocking collectives, per_device(): forcing = lax.all_gather(forcing, 'z', axis=0, tiled=True)  27.2 us
    all_to_all x1, blocking collectives, per_device(): lax.all_to_all(parts, 'z', 0, 0, tiled=True, axis_index_groups=NEAR_GROUPS)  13.7 us
    all_to_all x1, blocking collectives, per_device(): back = lax.all_to_all(back, ('pair', 'chip'), 0, 0, tiled=True)  12.8 us
    ppermute x1, starting transfers between devices, per_device(): got = lax.ppermute(give, 'core', SWAP)  10.8 us
    all_to_all x1, starting transfers between devices, per_device(): lax.all_to_all(own_control, ('pair', 'chip', 'core'), 0, 0, tiled=True)  8.52 us
    all_to_all x1, waiting for transfers between devices, per_device(): lax.all_to_all(own_control, ('pair', 'chip', 'core'), 0, 0, tiled=True)  7.83 us
  transfers between devices with their start and end apart: 3, of which 2 were waited for; matrix products, arithmetic and copies ran while one was open for 1% of the time, Pallas kernels for 0%

profile of v3, /device:TPU:1, one launch (start us, length us, event | category | flops | bytes accessed | tf_op | source)
XLA Modules:
  0.0 173.1 jit_solution(17058712487185391447)
XLA Ops:
  0.6 0.0 copy-start.4
  0.6 4.9 %shard_map.77 = (bf16[4,1536,128]{2,1,0:T(8,128)(2,1)}, bf16[4,1536,128]{2,1,0:T(8,128)(2,1)}, bf16[96,256]{1,0:T(8,128)(2,1)}) custom-call(bf16[512,3072]{1,0:T(8,128)(2,1)} %bitcast.20, bf16[96,256]{1,0:T(8,128)(2,1)} %lon_ref.1), custom_call_target="tpu_custom_call" | custom-call | tf_op jit(solution)/shard_map/pallas_call | solution.py:128
  5.5 4.0 %collective-permute-start = (bf16[4,1536,128]{2,1,0:T(8,128)(2,1)}, bf16[4,1536,128]{2,1,0:T(8,128)(2,1)}, u32[]{:S(2)}, u32[]{:S(2)}) collective-permute-start(bf16[4,1536,128]{2,1,0:T(8,128)(2,1)} %get-tuple-element.10), channel_id=1, source_target_pairs={{0,16},{16,0},{1,17},{17,1},{2,18},{18,2},{3,19},{19,3},{4,20},{20... | collective-permute-start | bytes 4718600 | tf_op jit(solution)/shard_map/ppermute | solution.py:137
  9.5 0.0 copy-done.4
  9.5 0.0 copy-start.5
  9.5 1.1 broadcast_in_dim.3
  10.7 0.0 copy-start
  10.7 0.0 copy-start.1
  10.7 8.5 %all-to-all-start = ((bf16[32,8,2048]{2,1,0:T(8,128)(2,1)}), bf16[32,8,2048]{2,1,0:T(8,128)(2,1)S(1)}, u32[]{:S(2)}, u32[]{:S(2)}) async-start(bf16[32,8,2048]{2,1,0:T(8,128)(2,1)} %broadcast_in_dim.3), calls=%async_computation | async-start | bytes 2097152 | tf_op jit(solution)/shard_map/all_to_all | solution.py:139
  19.2 0.0 copy-done.5
  19.2 33.3 %all_gather.6.lon_ref = bf16[1536,256]{1,0:T(8,128)(2,1)S(1)} all-gather(bf16[96,256]{1,0:T(8,128)(2,1)S(1)} %copy-done.5), channel_id=1, replica_groups=mesh['z'=16,'pair'=2,'chip'=8,'core'=2] {'z'}, dimensions={0}, use_global_device_ids=true | all-gather | bytes 835584 | tf_op jit(solution)/shard_map/all_gather | solution.py:138
  52.5 7.8 %all-to-all-done = bf16[32,8,2048]{2,1,0:T(8,128)(2,1)S(1)} async-done(((bf16[32,8,2048]{2,1,0:T(8,128)(2,1)}), bf16[32,8,2048]{2,1,0:T(8,128)(2,1)S(1)}, u32[]{:S(2)}, u32[]{:S(2)}) %all-to-all-start) | async-done | bytes 1048608 | tf_op jit(solution)/shard_map/all_to_all | solution.py:139
  60.3 0.0 collective-permute-done.traded_ref
  60.3 0.0 copy-done
  60.3 0.0 copy-done.1
  60.3 3.7 %shard_map.78 = bf16[2,8,96,256]{3,2,1,0:T(8,128)(2,1)S(1)} custom-call(bf16[4,1536,128]{2,1,0:T(8,128)(2,1)S(1)} %copy-done, bf16[4,1536,128]{2,1,0:T(8,128)(2,1)} %collective-permute-done.traded_ref, bf16[256,2048]{1,0:T(8,128)(2,1)S(1)} %bitcast.16, bf16[64,128]{1,0:T(8,128)(2,1)S(1)} %copy-done.1, bf16[1536,256]{1,0:T(8,128)(2,1)S(1)} %all_gather.6.lon_ref), custom_call_target="tpu_custom_call" | custom-call | tf_op jit(solution)/shard_map/pallas_call | solution.py:141
  64.1 0.0 copy-start.2
  64.1 0.0 copy-start.3
  64.1 13.7 %all_to_all.27 = bf16[2,8,96,256]{3,2,1,0:T(8,128)(2,1)S(1)} all-to-all(bf16[2,8,96,256]{3,2,1,0:T(8,128)(2,1)S(1)} %shard_map.78), channel_id=1, replica_groups={{0,32},{64,96},{128,160},{192,224},{256,288},{320,352},{384,416},{448,4..., dimensions={0} | all-to-all | bytes 1572864 | tf_op jit(solution)/shard_map/all_to_all | solution.py:151
  77.8 1.0 reduce_sum.21
  78.8 36.5 %all_to_all.28.refs_0_ = bf16[8,96,256]{2,1,0:T(8,128)(2,1)S(1)} all-to-all(bf16[8,96,256]{2,1,0:T(8,128)(2,1)} %reduce_sum.21), channel_id=1, replica_groups={{0,256,128,384,64,320,192,448},{32,288,160,416,96,352,224,480},{1,257,1..., dimensions={0} | all-to-all | bytes 786432 | tf_op jit(solution)/shard_map/all_to_all | solution.py:153
  115.3 0.0 copy-done.2
  115.3 0.0 copy-done.3
  115.3 0.8 shard_map.79
  116.1 27.2 %all_gather.7.forcing_ref = bf16[1536,256]{1,0:T(8,128)(2,1)S(1)} all-gather(bf16[96,256]{1,0:T(8,128)(2,1)S(1)} %get-tuple-element.13), channel_id=1, replica_groups=mesh['z'=16,'pair'=2,'chip'=8,'core'=2] {'z'}, dimensions={0}, use_global_device_ids=true | all-gather | bytes 835584 | tf_op jit(solution)/shard_map/all_gather | solution.py:159
  143.3 3.8 %shard_map.80 = (f32[128,2048]{1,0:T(8,128)S(1)}, bf16[128,2048]{1,0:T(8,128)(2,1)S(1)}) custom-call(bf16[4,1536,128]{2,1,0:T(8,128)(2,1)S(1)} %copy-done, bf16[4,1536,128]{2,1,0:T(8,128)(2,1)} %collective-permute-done.traded_ref, bf16[1536,256]{1,0:T(8,128)(2,1)S(1)} %all_gather.7.forcing_ref, bf16[64,128]{1,0:T(8,128)(2,1)S(1)} %copy-done.1, ...), custom_call_target="tpu_custom_call" | custom-call | tf_op jit(solution)/shard_map/pallas_call | solution.py:161
  147.1 10.8 %collective-permute-start.1 = (bf16[128,2048]{1,0:T(8,128)(2,1)S(1)}, bf16[128,2048]{1,0:T(8,128)(2,1)S(1)}, u32[]{:S(2)}, u32[]{:S(2)}) collective-permute-start(bf16[128,2048]{1,0:T(8,128)(2,1)S(1)} %get-tuple-element.15), channel_id=1, source_target_pairs={{0,1},{1,0},{2,3},{3,2},{4,5},{5,4},{6,7},{7,6},{8,9},{9,8},{10,11... | collective-permute-start | bytes 1572872 | tf_op jit(solution)/shard_map/ppermute | solution.py:170
  157.9 1.5 collective-permute-done.1.got_ref
  159.4 0.1 shard_map.81
  159.5 12.8 %all_to_all.29 = bf16[16,8,2048]{2,1,0:T(8,128)(2,1)S(1)} all-to-all(bf16[16,8,2048]{2,1,0:T(8,128)(2,1)S(1)} %bitcast.17), channel_id=1, replica_groups=mesh['z'=16,'pair'=2,'chip'=8,'core'=2] {'pair','chip'}, dimensions={0} | all-to-all | bytes 1048576 | tf_op jit(solution)/shard_map/all_to_all | solution.py:172
  172.4 0.1 convert_reduce_fusion
  172.4 0.6 add.3
  (2 shorter events, 0.0 us)
Async XLA Ops:
  0.6 8.9 %copy-start.4 = (f32[2,2,2,8,256]{4,3,2,1,0:T(8,128)S(1)}, f32[2,2,2,8,256]{4,3,2,1,0:T(8,128)}, u32[]{:S(2)}) copy-start(f32[2,2,2,8,256]{4,3,2,1,0:T(8,128)} %param.7) | copy-start | bytes 196612
  5.5 54.8 %collective-permute-start = (bf16[4,1536,128]{2,1,0:T(8,128)(2,1)}, bf16[4,1536,128]{2,1,0:T(8,128)(2,1)}, u32[]{:S(2)}, u32[]{:S(2)}) collective-permute-start(bf16[4,1536,128]{2,1,0:T(8,128)(2,1)} %get-tuple-element.10), channel_id=1, source_target_pairs={{0,16},{16,0},{1,17},{17,1},{2,18},{18,2},{3,19},{19,3},{4,20},{20... | collective-permute-start | bytes 4718600 | tf_op jit(solution)/shard_map/ppermute | solution.py:137
  9.5 9.7 %copy-start.5 = (bf16[96,256]{1,0:T(8,128)(2,1)S(1)}, bf16[96,256]{1,0:T(8,128)(2,1)}, u32[]{:S(2)}) copy-start(bf16[96,256]{1,0:T(8,128)(2,1)} %get-tuple-element.11) | copy-start | bytes 147460
  10.7 49.6 %copy-start = (bf16[4,1536,128]{2,1,0:T(8,128)(2,1)S(1)}, bf16[4,1536,128]{2,1,0:T(8,128)(2,1)}, u32[]{:S(2)}) copy-start(bf16[4,1536,128]{2,1,0:T(8,128)(2,1)} %get-tuple-element.9.own_ref) | copy-start | bytes 4718596
  10.7 49.6 %copy-start.1 = (bf16[64,128]{1,0:T(8,128)(2,1)S(1)}, bf16[64,128]{1,0:T(8,128)(2,1)}, u32[]{:S(2)}) copy-start(bf16[64,128]{1,0:T(8,128)(2,1)} %lat_ref.3) | copy-start | bytes 49156
  10.7 49.6 %all-to-all-start = ((bf16[32,8,2048]{2,1,0:T(8,128)(2,1)}), bf16[32,8,2048]{2,1,0:T(8,128)(2,1)S(1)}, u32[]{:S(2)}, u32[]{:S(2)}) async-start(bf16[32,8,2048]{2,1,0:T(8,128)(2,1)} %broadcast_in_dim.3), calls=%async_computation | async-start | bytes 2097152 | tf_op jit(solution)/shard_map/all_to_all | solution.py:139
  64.1 51.3 %copy-start.2 = (bf16[2,2,64,96]{3,2,1,0:T(8,128)(2,1)S(1)}, bf16[2,2,64,96]{3,2,1,0:T(8,128)(2,1)}, u32[]{:S(2)}) copy-start(bf16[2,2,64,96]{3,2,1,0:T(8,128)(2,1)} %param.10) | copy-start | bytes 147460
  64.1 51.3 %copy-start.3 = (bf16[2,2,64,96]{3,2,1,0:T(8,128)(2,1)S(1)}, bf16[2,2,64,96]{3,2,1,0:T(8,128)(2,1)}, u32[]{:S(2)}) copy-start(bf16[2,2,64,96]{3,2,1,0:T(8,128)(2,1)} %param.11) | copy-start | bytes 147460
  147.1 12.3 %collective-permute-start.1 = (bf16[128,2048]{1,0:T(8,128)(2,1)S(1)}, bf16[128,2048]{1,0:T(8,128)(2,1)S(1)}, u32[]{:S(2)}, u32[]{:S(2)}) collective-permute-start(bf16[128,2048]{1,0:T(8,128)(2,1)S(1)} %get-tuple-element.15), channel_id=1, source_target_pairs={{0,1},{1,0},{2,3},{3,2},{4,5},{5,4},{6,7},{7,6},{8,9},{9,8},{10,11... | collective-permute-start | bytes 1572872 | tf_op jit(solution)/shard_map/ppermute | solution.py:170

commit v4 on v3

v4 whole, which is shorter than its diff:
```python
import math

import jax
import jax.numpy as jnp
from jax import lax
from jax.experimental import pallas as pl
from jax.experimental.pallas import tpu as pltpu
from jax.sharding import Mesh, PartitionSpec as P

PAIR, RING, CHIPS, CORES, FAR = 2, 16, 8, 2, 8
ORDER = (0, 4, 2, 6, 1, 5, 3, 7)
FAR_GROUPS = [[2 * far + parity for far in ORDER] for parity in range(2)]
SWAP = [(0, 1), (1, 0)]
F32, BF16 = jnp.float32, jnp.bfloat16


def place(far):
    return ((far & 1) << 2) | (far & 2) | (far >> 2)


def z_parity():
    return lax.axis_index("z") & 1


def half_basis(lat_ref, core):
    held = lax.broadcasted_iota(jnp.int32, (128, 64), 0)
    wanted = lax.broadcasted_iota(jnp.int32, (128, 64), 1)
    wanted = ((wanted >> 3) << 4) + (wanted & 7) + 8 * core
    pick = jnp.where(held == wanted, 1.0, 0.0).astype(BF16)
    return jnp.dot(lat_ref[...], pick, preferred_element_type=F32).astype(BF16)


def columns(perturb_ref, turned_ref, outs):
    turned_ref[...] = perturb_ref[...].astype(F32).T.astype(BF16)
    parity = z_parity()
    for pair, out_ref in outs:
        for half in range(2):
            for far in range(FAR):
                row = 96 * (FAR * half + far)
                start = pl.multiple_of(384 * far + 192 * (1 - half ^ parity) + 96 * pair, 96)
                out_ref[0, row : row + 96, :] = turned_ref[pl.ds(start, 96), :]


def first_kernel(perturb_ref, first_ref, turned_ref):
    columns(perturb_ref, turned_ref, [(1 - lax.axis_index("pair"), first_ref)])


def columns_kernel(perturb_ref, lon_ref, before_ref, own_ref, second_ref, copy_ref, turned_ref):
    copy_ref[...] = lon_ref[...]
    me = lax.axis_index("pair")

    @pl.when(pl.program_id(0) < 2)
    def _():
        columns(perturb_ref, turned_ref, [(1 - me, second_ref), (me, own_ref)])

    @pl.when(pl.program_id(0) >= 2)
    def _():
        columns(perturb_ref, turned_ref, [(me, own_ref)])


def perturb_block(own_ref, first_ref, second_ref, other, block):
    if other == 0:
        return own_ref[block].astype(F32)
    return (first_ref, second_ref)[block // 2][block % 2].astype(F32)


def terms(own_ref, first_ref, second_ref, part_ref, lon):
    me = lax.axis_index("pair")
    halves = [jnp.zeros((192, 128), F32), jnp.zeros((192, 128), F32)]
    for other in range(PAIR):
        field = lax.dot_general(
            lon, part_ref[me ^ other], (((1,), (1,)), ((), ())), preferred_element_type=F32
        )
        for block in range(4):
            perturb = perturb_block(own_ref, first_ref, second_ref, other, block)
            halves[block % 2] += perturb * field[:, 128 * block : 128 * block + 128]
    return halves


def store_terms(halves, out_ref):
    step = pl.program_id(0)
    for half in range(2):
        total = halves[half].astype(out_ref.dtype)
        for i in range(2):
            out_ref[place(2 * step + i), :, 128 * half : 128 * half + 128] = total[96 * i : 96 * i + 96]


def forward_kernel(own_ref, first_ref, second_ref, control_ref, lat_ref, lon_ref, out_ref, part_ref):
    @pl.when(pl.program_id(0) == 0)
    def _():
        for pair in range(PAIR):
            control = control_ref[128 * pair : 128 * pair + 128, :]
            lat_part = jnp.dot(lat_ref[...], control, preferred_element_type=F32).astype(BF16)
            for g in range(8):
                part_ref[pair, 64 * g : 64 * g + 64, :] = lat_part[:, 256 * g : 256 * g + 256]

    lon = lon_ref[:, 1 - z_parity()].reshape(192, 256)
    store_terms(terms(own_ref, first_ref, second_ref, part_ref, lon), out_ref)


def forward_own_kernel(own_ref, first_ref, second_ref, part_ref, lon_ref, out_ref):
    lon = lon_ref[:, z_parity()].reshape(192, 256)
    store_terms(terms(own_ref, first_ref, second_ref, part_ref, lon), out_ref)


def forcing_kernel(factor, parts_ref, innovation_ref, weights_ref, increment_ref, forcing_ref):
    summed = jnp.sum(parts_ref[...].astype(F32), axis=0) * factor
    increment = summed.T
    increment_ref[...] = increment
    forcing = weights_ref[...].astype(F32) * (increment - innovation_ref[...].astype(F32))
    forcing_ref[...] = forcing.T.astype(BF16)


def backward_kernel(own_ref, first_ref, second_ref, forcing_ref, lat_ref, lon_ref, keep_ref, give_ref, total_ref):
    step = pl.program_id(0)

    @pl.when(step == 0)
    def _():
        total_ref[...] = jnp.zeros_like(total_ref)

    half = jnp.where(step < 2, 1, 0) ^ z_parity()
    lon = lon_ref[:, half].reshape(384, 256)
    forcing = forcing_ref[:, half].reshape(384, 256).astype(F32)
    for other in range(PAIR):
        for block in range(4):
            lanes = slice(128 * (block % 2), 128 * (block % 2) + 128)
            perturb = perturb_block(own_ref, first_ref, second_ref, other, block)
            weighted = (perturb * forcing[:, lanes]).astype(BF16)
            total_ref[other, 128 * block : 128 * block + 128, :] += lax.dot_general(
                weighted, lon, (((0,), (0,)), ((), ())), preferred_element_type=F32
            )

    @pl.when(step == pl.num_programs(0) - 1)
    def _():
        me, core = lax.axis_index("pair"), lax.axis_index("core")
        lat_mine, lat_swapped = half_basis(lat_ref, core), half_basis(lat_ref, 1 - core)
        for other in range(PAIR):
            rows = pl.ds(pl.multiple_of(64 * (me ^ other), 64), 64)
            lon_back = total_ref[other].astype(BF16)
            for g in range(8):
                part = lon_back[64 * g : 64 * g + 64]
                for lat, out_ref in ((lat_mine, keep_ref), (lat_swapped, give_ref)):
                    out_ref[rows, 256 * g : 256 * g + 256] = lax.dot_general(
                        lat, part, (((0,), (0,)), ((), ())), preferred_element_type=F32
                    ).astype(out_ref.dtype)


def add_kernel(keep_ref, got_ref, out_ref):
    out_ref[...] = (keep_ref[...] + got_ref[...].astype(F32)).astype(BF16)


def gradient_kernel(factor, back_ref, control_ref, out_ref):
    back = jnp.sum(back_ref[...].astype(F32).reshape(PAIR * CHIPS, 8, 2048), axis=0) * factor
    for g in range(8):
        rows = slice(8 * g, 8 * g + 8)
        out_ref[rows, :] = control_ref[rows, :] + back[:, 256 * g : 256 * g + 256]


def whole(*shape):
    return pl.BlockSpec(shape, lambda step: (0,) * len(shape))


def rows_of(*shape):
    return pl.BlockSpec(shape, lambda step: (0,) * (len(shape) - 2) + (step, 0))


def shape_of(shape, dtype=BF16):
    return jax.ShapeDtypeStruct(shape, dtype)


def per_device(perturb, control, lat_basis, lon_basis, innovation, weights):
    factor = 1.0 / math.sqrt(63)
    params = pltpu.CompilerParams(vmem_limit_bytes=20 * 2**20)

    own_control = control.reshape(8, 8, 256).transpose(1, 0, 2).reshape(8, 2048).astype(BF16)
    own_control = jnp.broadcast_to(own_control, (PAIR * CHIPS * CORES, 8, 2048)).reshape(256, 2048)
    large = pltpu.CompilerParams(vmem_limit_bytes=60 * 2**20)
    perturb = perturb.reshape(512, 3072)

    def block_of(index):
        return pl.BlockSpec((1, 1536, 128), lambda step: (index(step), 0, 0))

    first = pl.pallas_call(
        first_kernel,
        grid=(2,),
        in_specs=[rows_of(128, 3072)],
        out_specs=block_of(lambda step: step),
        out_shape=shape_of((2, 1536, 128)),
        scratch_shapes=[pltpu.VMEM((3072, 128), BF16)],
        compiler_params=large,
    )(perturb)
    own, second, lon = pl.pallas_call(
        columns_kernel,
        grid=(4,),
        in_specs=[
            pl.BlockSpec((128, 3072), lambda step: (step ^ 2, 0)),
            whole(96, 256),
            pl.BlockSpec(memory_space=pl.ANY),
        ],
        out_specs=[
            block_of(lambda step: step ^ 2),
            block_of(lambda step: jnp.minimum(step, 1)),
            whole(96, 256),
        ],
        out_shape=[shape_of((4, 1536, 128)), shape_of((2, 1536, 128)), shape_of((96, 256))],
        scratch_shapes=[pltpu.VMEM((3072, 128), BF16)],
        compiler_params=large,
    )(perturb, lon_basis, first)
    first = lax.ppermute(first, "pair", SWAP)
    second = lax.ppermute(second, "pair", SWAP)
    lon = lax.all_gather(lon, "z", axis=0, tiled=True)
    full_control = lax.all_to_all(own_control, ("pair", "chip", "core"), 0, 0, tiled=True)

    lon = lon.reshape(FAR, 2, 96, 256)

    def later(*shape):
        return pl.BlockSpec(shape, lambda step: (0, step + 4, 0))

    lon_spec = pl.BlockSpec((2, 2, 96, 256), lambda step: (step, 0, 0, 0))
    give, lat_part = pl.pallas_call(
        forward_kernel,
        grid=(4,),
        in_specs=[rows_of(4, 192, 128), rows_of(2, 192, 128), rows_of(2, 192, 128)]
        + [whole(256, 2048), whole(64, 128), lon_spec],
        out_specs=[whole(FAR, 96, 256), whole(PAIR, 512, 256)],
        out_shape=[shape_of((FAR, 96, 256)), shape_of((PAIR, 512, 256))],
        compiler_params=params,
    )(own, first, second, full_control, lat_basis, lon)
    got = lax.ppermute(give, "z", [(z, z ^ 1) for z in range(RING)])
    keep = pl.pallas_call(
        forward_own_kernel,
        grid=(4,),
        in_specs=[later(4, 192, 128), later(2, 192, 128), later(2, 192, 128)]
        + [whole(PAIR, 512, 256), lon_spec],
        out_specs=whole(FAR, 96, 256),
        out_shape=shape_of((FAR, 96, 256), F32),
        compiler_params=params,
    )(own, first, second, lat_part, lon)
    parts = pl.pallas_call(add_kernel, out_shape=shape_of((FAR, 96, 256)), compiler_params=params)(keep, got)
    parts = lax.all_to_all(parts, "z", 0, 0, tiled=True, axis_index_groups=FAR_GROUPS)
    increment, forcing = pl.pallas_call(
        lambda *refs: forcing_kernel(factor, *refs),
        out_shape=(shape_of((256, 96), F32), shape_of((96, 256))),
        compiler_params=params,
    )(parts, innovation.reshape(256, 96), weights.reshape(256, 96))
    forcing = lax.all_gather(forcing, "z", axis=0, tiled=True).reshape(FAR, 2, 96, 256)
    half_spec = pl.BlockSpec((4, 2, 96, 256), lambda step: (lax.rem(step, 2), 0, 0, 0))

    keep, give = pl.pallas_call(
        backward_kernel,
        grid=(4,),
        in_specs=[rows_of(4, 384, 128), rows_of(2, 384, 128), rows_of(2, 384, 128)]
        + [half_spec, whole(64, 128), half_spec],
        out_specs=[whole(128, 2048)] * 2,
        out_shape=[shape_of((128, 2048), F32), shape_of((128, 2048))],
        scratch_shapes=[pltpu.VMEM((PAIR, 512, 256), F32)],
        compiler_params=params,
    )(own, first, second, forcing, lat_basis, lon)
    got = lax.ppermute(give, "core", SWAP)
    back = pl.pallas_call(add_kernel, out_shape=shape_of((128, 2048)), compiler_params=params)(keep, got)
    back = lax.all_to_all(back, ("pair", "chip"), 0, 0, tiled=True)
    gradient = pl.pallas_call(
        lambda *refs: gradient_kernel(factor, *refs),
        out_shape=shape_of((64, 256), F32),
        compiler_params=params,
    )(back, control.reshape(64, 256))
    return (increment.reshape(innovation.shape), gradient.reshape(control.shape))


def solution(mesh):
    members, space = ("z", "pair"), ("chip", "core")
    devices = mesh.devices.reshape(RING, PAIR, CHIPS, CORES)
    return jax.shard_map(
        per_device,
        mesh=Mesh(devices, (*members, *space)),
        in_specs=(
            P(members, None, None, space, None),
            P(members, None, None, space, None),
            P(space, None),
            P(members, None),
            P(None, None, space, members),
            P(None, None, space, members),
        ),
        out_specs=(P(None, None, space, members), P(members, None, None, space, None)),
        check_vma=False,
    )
```

time: 174 us -> 171 us (0.983)
  blocking collectives: 124 us -> 114 us
  starting transfers between devices: 23.3 us -> 28.3 us
  Pallas kernels: 13.3 us -> 15.4 us
    all_to_all x1 -> x0, blocking collectives: 13.7 us -> none  [per_device(): lax.all_to_all(parts, 'z', 0, 0, tiled=True, axis_index_groups=NEAR_GROUPS)]
    all_to_all x1, waiting for transfers between devices: 7.83 us -> 0.01 us  [per_device(): lax.all_to_all(own_control, ('pair', 'chip', 'core'), 0, 0, tiled=True)]
    ppermute x1 -> x3, waiting for transfers between devices: 0.01 us -> 7.48 us  [the longest x1 4.97 us: per_device(): got = lax.ppermute(give, 'z', [(z, z ^ 1) for z in range(RING)])]
    all_to_all x1, blocking collectives: 12.8 us -> 16.2 us  [per_device(): back = lax.all_to_all(back, ('pair', 'chip'), 0, 0, tiled=True)]
    ppermute x1 -> x3, starting transfers between devices: 3.98 us -> 7.35 us  [the longest x1 3.51 us: per_device(): first = lax.ppermute(first, 'pair', SWAP)]
    all_gather x1, blocking collectives: 27.2 us -> 29.7 us  [per_device(): lax.all_gather(forcing, 'z', axis=0, tiled=True).reshape(FAR, 2, 96, 256)]
    pallas_call x3 -> x7, Pallas kernels: 12.4 us -> 14.5 us  [the longest x1 4.78 us: per_device(): pl.pallas_call(columns_kernel, grid=(4,), in_specs=[pl.BlockSpec((128, 30...]
    all_to_all x1, starting transfers between devices: 8.52 us -> 10.5 us  [per_device(): lax.all_to_all(own_control, ('pair', 'chip', 'core'), 0, 0, tiled=True)]
  transfers between devices with their start and end apart: 3 -> 5, of which waited for: 2 -> 3; matrix products, arithmetic and copies ran while one was open for 1% -> 0% of each run, Pallas kernels for 0% -> 5%
where the time goes in v4:
time: 171 us
  blocking collectives  114 us (67%)
  starting transfers between devices  28.3 us (17%)
  Pallas kernels  15.4 us (9%)
  waiting for transfers between devices  9 us (5%)
  local copies, waits for them, and re-layouts  2.54 us (1%)
    all_to_all x1, blocking collectives, per_device(): lax.all_to_all(parts, 'z', 0, 0, tiled=True, axis_index_groups=FAR_GROUPS)  35.9 us
    all_gather x1, blocking collectives, per_device(): lon = lax.all_gather(lon, 'z', axis=0, tiled=True)  32 us
    all_gather x1, blocking collectives, per_device(): lax.all_gather(forcing, 'z', axis=0, tiled=True).reshape(FAR, 2, 96, 256)  29.7 us
    all_to_all x1, blocking collectives, per_device(): back = lax.all_to_all(back, ('pair', 'chip'), 0, 0, tiled=True)  16.2 us
    ppermute x1, starting transfers between devices, per_device(): got = lax.ppermute(give, 'core', SWAP)  10.5 us
    all_to_all x1, starting transfers between devices, per_device(): lax.all_to_all(own_control, ('pair', 'chip', 'core'), 0, 0, tiled=True)  10.5 us
    ppermute x1, waiting for transfers between devices, per_device(): got = lax.ppermute(give, 'z', [(z, z ^ 1) for z in range(RING)])  4.97 us
    pallas_call x1, Pallas kernels, per_device(): pl.pallas_call(columns_kernel, grid=(4,), in_specs=[pl.BlockSpec((128, 30...  4.78 us
  transfers between devices with their start and end apart: 5, of which 3 were waited for; matrix products, arithmetic and copies ran while one was open for 0% of the time, Pallas kernels for 5%

profile of v4, /device:TPU:1, one launch (start us, length us, event | category | flops | bytes accessed | tf_op | source)
XLA Modules:
  0.0 170.6 jit_solution(6236002657841354189)
XLA Ops:
  0.6 0.8 convert_element_type.12
  1.5 1.1 broadcast_in_dim.3
  2.6 10.5 %all-to-all-start = ((bf16[32,8,2048]{2,1,0:T(8,128)(2,1)}), bf16[32,8,2048]{2,1,0:T(8,128)(2,1)S(1)}, u32[]{:S(2)}, u32[]{:S(2)}) async-start(bf16[32,8,2048]{2,1,0:T(8,128)(2,1)} %broadcast_in_dim.3), calls=%async_computation | async-start | bytes 2097152 | tf_op jit(solution)/shard_map/all_to_all | solution.py:212
  13.1 2.5 %shard_map.77.before_ref = bf16[2,1536,128]{2,1,0:T(8,128)(2,1)} custom-call(bf16[512,3072]{1,0:T(8,128)(2,1)} %bitcast.26), custom_call_target="tpu_custom_call" | custom-call | tf_op jit(solution)/shard_map/pallas_call | solution.py:183
  15.6 0.0 copy-start.3
  15.6 3.5 %collective-permute-start = (bf16[2,1536,128]{2,1,0:T(8,128)(2,1)}, bf16[2,1536,128]{2,1,0:T(8,128)(2,1)S(1)}, u32[]{:S(2)}, u32[]{:S(2)}) collective-permute-start(bf16[2,1536,128]{2,1,0:T(8,128)(2,1)} %shard_map.77.before_ref), channel_id=1, source_target_pairs={{0,16},{16,0},{1,17},{17,1},{2,18},{18,2},{3,19},{19,3},{4,20},{20... | collective-permute-start | bytes 2359304 | tf_op jit(solution)/shard_map/ppermute | solution.py:209
  19.1 4.8 %shard_map.78 = (bf16[4,1536,128]{2,1,0:T(8,128)(2,1)}, bf16[2,1536,128]{2,1,0:T(8,128)(2,1)}, bf16[96,256]{1,0:T(8,128)(2,1)}) custom-call(bf16[512,3072]{1,0:T(8,128)(2,1)} %bitcast.27, bf16[96,256]{1,0:T(8,128)(2,1)} %lon_ref.1, bf16[2,1536,128]{2,1,0:T(8,128)(2,1)} %shard_map.77.before_ref), custom_call_target="tpu_custom_call" | custom-call | tf_op jit(solution)/shard_map/pallas_call | solution.py:192
  23.9 1.9 %collective-permute-start.1 = (bf16[2,1536,128]{2,1,0:T(8,128)(2,1)}, bf16[2,1536,128]{2,1,0:T(8,128)(2,1)S(1)}, u32[]{:S(2)}, u32[]{:S(2)}) collective-permute-start(bf16[2,1536,128]{2,1,0:T(8,128)(2,1)} %get-tuple-element.12), channel_id=1, source_target_pairs={{0,16},{16,0},{1,17},{17,1},{2,18},{18,2},{3,19},{19,3},{4,20},{20... | collective-permute-start | bytes 2359304 | tf_op jit(solution)/shard_map/ppermute | solution.py:210
  25.8 32.0 %all_gather.6 = bf16[1536,256]{1,0:T(8,128)(2,1)S(1)} all-gather(bf16[96,256]{1,0:T(8,128)(2,1)} %get-tuple-element.13), channel_id=1, replica_groups=mesh['z'=16,'pair'=2,'chip'=8,'core'=2] {'z'}, dimensions={0}, use_global_device_ids=true | all-gather | bytes 835584 | tf_op jit(solution)/shard_map/all_gather | solution.py:211
  57.8 0.0 collective-permute-done.first_ref
  57.8 2.5 %collective-permute-done.1.second_ref = bf16[2,1536,128]{2,1,0:T(8,128)(2,1)S(1)} collective-permute-done((bf16[2,1536,128]{2,1,0:T(8,128)(2,1)}, bf16[2,1536,128]{2,1,0:T(8,128)(2,1)S(1)}, u32[]{:S(2)}, u32[]{:S(2)}) %collective-permute-start.1) | collective-permute-done | bytes 786464 | tf_op jit(solution)/shard_map/ppermute | solution.py:210
  60.3 0.0 all-to-all-done
  60.3 0.0 copy-done.3
  60.4 0.0 copy-start
  60.4 1.4 copy-done
  61.8 1.9 %shard_map.79 = (bf16[8,96,256]{2,1,0:T(8,128)(2,1)S(1)}, bf16[2,512,256]{2,1,0:T(8,128)(2,1)S(1)}) custom-call(bf16[4,1536,128]{2,1,0:T(8,128)(2,1)S(1)} %copy-done, bf16[2,1536,128]{2,1,0:T(8,128)(2,1)S(1)} %collective-permute-done.first_ref, bf16[2,1536,128]{2,1,0:T(8,128)(2,1)S(1)} %collective-permute-done.1.second_ref, bf16[256,2048]{1,0:T(8,128)(2,1)S(1)} %bitcast.19, ...), custom_call_target="tpu_custom_call" | custom-call | tf_op jit(solution)/shard_map/pallas_call | solution.py:220
  63.7 1.9 %collective-permute-start.2 = (bf16[8,96,256]{2,1,0:T(8,128)(2,1)S(1)}, bf16[8,96,256]{2,1,0:T(8,128)(2,1)S(1)}, u32[]{:S(2)}, u32[]{:S(2)}) collective-permute-start(bf16[8,96,256]{2,1,0:T(8,128)(2,1)S(1)} %get-tuple-element.15), channel_id=1, source_target_pairs={{0,32},{32,0},{64,96},{96,64},{128,160},{160,128},{192,224},{224,1... | collective-permute-start | bytes 1179656 | tf_op jit(solution)/shard_map/ppermute | solution.py:229
  65.6 0.0 copy-start.4
  65.6 0.0 copy-start.5
  65.6 1.6 shard_map.80.keep_ref
  67.2 0.0 copy-start.1
  67.2 5.0 %collective-permute-done.2.got_ref = bf16[8,96,256]{2,1,0:T(8,128)(2,1)S(1)} collective-permute-done((bf16[8,96,256]{2,1,0:T(8,128)(2,1)S(1)}, bf16[8,96,256]{2,1,0:T(8,128)(2,1)S(1)}, u32[]{:S(2)}, u32[]{:S(2)}) %collective-permute-start.2) | collective-permute-done | bytes 393248 | tf_op jit(solution)/shard_map/ppermute | solution.py:229
  72.2 0.1 shard_map.81
  72.3 35.9 %all_to_all.24.refs_0_ = bf16[8,96,256]{2,1,0:T(8,128)(2,1)S(1)} all-to-all(bf16[8,96,256]{2,1,0:T(8,128)(2,1)S(1)} %shard_map.81), channel_id=1, replica_groups={{0,256,128,384,64,320,192,448},{32,288,160,416,96,352,224,480},{1,257,1..., dimensions={0} | all-to-all | bytes 786432 | tf_op jit(solution)/shard_map/all_to_all | solution.py:240
  108.1 0.0 copy-done.4
  108.1 0.0 copy-done.5
  108.1 0.8 shard_map.82
  108.9 29.7 %all_gather.7 = bf16[1536,256]{1,0:T(8,128)(2,1)S(1)} all-gather(bf16[96,256]{1,0:T(8,128)(2,1)S(1)} %get-tuple-element.17), channel_id=1, replica_groups=mesh['z'=16,'pair'=2,'chip'=8,'core'=2] {'z'}, dimensions={0}, use_global_device_ids=true | all-gather | bytes 835584 | tf_op jit(solution)/shard_map/all_gather | solution.py:246
  138.6 0.0 copy-done.1
  138.6 0.0 copy-start.2
  138.6 3.0 %shard_map.83 = (f32[128,2048]{1,0:T(8,128)S(1)}, bf16[128,2048]{1,0:T(8,128)(2,1)S(1)}) custom-call(bf16[4,1536,128]{2,1,0:T(8,128)(2,1)S(1)} %copy-done.1, bf16[2,1536,128]{2,1,0:T(8,128)(2,1)S(1)} %collective-permute-done.first_ref, bf16[2,1536,128]{2,1,0:T(8,128)(2,1)S(1)} %collective-permute-done.1.second_ref, bf16[8,2,96,256]{3,2,1,0:T(8,128)(2,1)S(1)} %bitcast.20, ...), custom_call_target="tpu_custom_call" | custom-call | tf_op jit(solution)/shard_map/pallas_call | solution.py:249
  141.6 10.5 %collective-permute-start.3 = (bf16[128,2048]{1,0:T(8,128)(2,1)S(1)}, bf16[128,2048]{1,0:T(8,128)(2,1)S(1)}, u32[]{:S(2)}, u32[]{:S(2)}) collective-permute-start(bf16[128,2048]{1,0:T(8,128)(2,1)S(1)} %get-tuple-element.19), channel_id=1, source_target_pairs={{0,1},{1,0},{2,3},{3,2},{4,5},{5,4},{6,7},{7,6},{8,9},{9,8},{10,11... | collective-permute-start | bytes 1572872 | tf_op jit(solution)/shard_map/ppermute | solution.py:259
  152.1 1.5 collective-permute-done.3.got_ref
  153.6 0.1 shard_map.84
  153.7 16.2 %all_to_all.25 = bf16[16,8,2048]{2,1,0:T(8,128)(2,1)S(1)} all-to-all(bf16[16,8,2048]{2,1,0:T(8,128)(2,1)S(1)} %bitcast.22), channel_id=1, replica_groups=mesh['z'=16,'pair'=2,'chip'=8,'core'=2] {'pair','chip'}, dimensions={0} | all-to-all | bytes 1048576 | tf_op jit(solution)/shard_map/all_to_all | solution.py:261
  169.9 0.0 copy-done.2
  169.9 0.7 shard_map.85
Async XLA Ops:
  2.6 57.8 %all-to-all-start = ((bf16[32,8,2048]{2,1,0:T(8,128)(2,1)}), bf16[32,8,2048]{2,1,0:T(8,128)(2,1)S(1)}, u32[]{:S(2)}, u32[]{:S(2)}) async-start(bf16[32,8,2048]{2,1,0:T(8,128)(2,1)} %broadcast_in_dim.3), calls=%async_computation | async-start | bytes 2097152 | tf_op jit(solution)/shard_map/all_to_all | solution.py:212
  15.6 44.8 %copy-start.3 = (bf16[64,128]{1,0:T(8,128)(2,1)S(1)}, bf16[64,128]{1,0:T(8,128)(2,1)}, u32[]{:S(2)}) copy-start(bf16[64,128]{1,0:T(8,128)(2,1)} %lat_ref.3) | copy-start | bytes 49156
  15.6 42.3 %collective-permute-start = (bf16[2,1536,128]{2,1,0:T(8,128)(2,1)}, bf16[2,1536,128]{2,1,0:T(8,128)(2,1)S(1)}, u32[]{:S(2)}, u32[]{:S(2)}) collective-permute-start(bf16[2,1536,128]{2,1,0:T(8,128)(2,1)} %shard_map.77.before_ref), channel_id=1, source_target_pairs={{0,16},{16,0},{1,17},{17,1},{2,18},{18,2},{3,19},{19,3},{4,20},{20... | collective-permute-start | bytes 2359304 | tf_op jit(solution)/shard_map/ppermute | solution.py:209
  23.9 36.5 %collective-permute-start.1 = (bf16[2,1536,128]{2,1,0:T(8,128)(2,1)}, bf16[2,1536,128]{2,1,0:T(8,128)(2,1)S(1)}, u32[]{:S(2)}, u32[]{:S(2)}) collective-permute-start(bf16[2,1536,128]{2,1,0:T(8,128)(2,1)} %get-tuple-element.12), channel_id=1, source_target_pairs={{0,16},{16,0},{1,17},{17,1},{2,18},{18,2},{3,19},{19,3},{4,20},{20... | collective-permute-start | bytes 2359304 | tf_op jit(solution)/shard_map/ppermute | solution.py:210
  60.4 1.4 copy-start
  63.7 8.5 %collective-permute-start.2 = (bf16[8,96,256]{2,1,0:T(8,128)(2,1)S(1)}, bf16[8,96,256]{2,1,0:T(8,128)(2,1)S(1)}, u32[]{:S(2)}, u32[]{:S(2)}) collective-permute-start(bf16[8,96,256]{2,1,0:T(8,128)(2,1)S(1)} %get-tuple-element.15), channel_id=1, source_target_pairs={{0,32},{32,0},{64,96},{96,64},{128,160},{160,128},{192,224},{224,1... | collective-permute-start | bytes 1179656 | tf_op jit(solution)/shard_map/ppermute | solution.py:229
  65.6 42.5 %copy-start.4 = (bf16[2,2,64,96]{3,2,1,0:T(8,128)(2,1)S(1)}, bf16[2,2,64,96]{3,2,1,0:T(8,128)(2,1)}, u32[]{:S(2)}) copy-start(bf16[2,2,64,96]{3,2,1,0:T(8,128)(2,1)} %param.10) | copy-start | bytes 147460
  65.6 42.5 %copy-start.5 = (bf16[2,2,64,96]{3,2,1,0:T(8,128)(2,1)S(1)}, bf16[2,2,64,96]{3,2,1,0:T(8,128)(2,1)}, u32[]{:S(2)}) copy-start(bf16[2,2,64,96]{3,2,1,0:T(8,128)(2,1)} %param.11) | copy-start | bytes 147460
  67.2 71.4 %copy-start.1 = (bf16[4,1536,128]{2,1,0:T(8,128)(2,1)S(1)}, bf16[4,1536,128]{2,1,0:T(8,128)(2,1)}, u32[]{:S(2)}) copy-start(bf16[4,1536,128]{2,1,0:T(8,128)(2,1)} %get-tuple-element.11.own_ref) | copy-start | bytes 4718596
  138.6 31.3 %copy-start.2 = (f32[2,2,2,8,256]{4,3,2,1,0:T(8,128)S(1)}, f32[2,2,2,8,256]{4,3,2,1,0:T(8,128)}, u32[]{:S(2)}) copy-start(f32[2,2,2,8,256]{4,3,2,1,0:T(8,128)} %param.7) | copy-start | bytes 196612
  141.6 12.0 %collective-permute-start.3 = (bf16[128,2048]{1,0:T(8,128)(2,1)S(1)}, bf16[128,2048]{1,0:T(8,128)(2,1)S(1)}, u32[]{:S(2)}, u32[]{:S(2)}) collective-permute-start(bf16[128,2048]{1,0:T(8,128)(2,1)S(1)} %get-tuple-element.19), channel_id=1, source_target_pairs={{0,1},{1,0},{2,3},{3,2},{4,5},{5,4},{6,7},{7,6},{8,9},{9,8},{10,11... | collective-permute-start | bytes 1572872 | tf_op jit(solution)/shard_map/ppermute | solution.py:259

commit v5 on v4

--- a/solution.py
+++ b/solution.py
@@ -11,6 +11,7 @@
 ORDER = (0, 4, 2, 6, 1, 5, 3, 7)
 FAR_GROUPS = [[2 * far + parity for far in ORDER] for parity in range(2)]
 SWAP = [(0, 1), (1, 0)]
+BACKWARD = [[RING - 1 - z for z in range(RING)]]
 F32, BF16 = jnp.float32, jnp.bfloat16
 
 
@@ -120,7 +121,7 @@
 
     half = jnp.where(step < 2, 1, 0) ^ z_parity()
     lon = lon_ref[:, half].reshape(384, 256)
-    forcing = forcing_ref[:, half].reshape(384, 256).astype(F32)
+    forcing = jnp.concatenate([forcing_ref[3 - far, 1 - half] for far in range(4)], axis=0).astype(F32)
     for other in range(PAIR):
         for block in range(4):
             lanes = slice(128 * (block % 2), 128 * (block % 2) + 128)
@@ -243,14 +244,15 @@
         out_shape=(shape_of((256, 96), F32), shape_of((96, 256))),
         compiler_params=params,
     )(parts, innovation.reshape(256, 96), weights.reshape(256, 96))
-    forcing = lax.all_gather(forcing, "z", axis=0, tiled=True).reshape(FAR, 2, 96, 256)
+    forcing = lax.all_gather(forcing, "z", axis=0, tiled=True, axis_index_groups=BACKWARD).reshape(FAR, 2, 96, 256)
     half_spec = pl.BlockSpec((4, 2, 96, 256), lambda step: (lax.rem(step, 2), 0, 0, 0))
+    turned_spec = pl.BlockSpec((4, 2, 96, 256), lambda step: (1 - lax.rem(step, 2), 0, 0, 0))
 
     keep, give = pl.pallas_call(
         backward_kernel,
         grid=(4,),
         in_specs=[rows_of(4, 384, 128), rows_of(2, 384, 128), rows_of(2, 384, 128)]
-        + [half_spec, whole(64, 128), half_spec],
+        + [turned_spec, whole(64, 128), half_spec],
         out_specs=[whole(128, 2048)] * 2,
         out_shape=[shape_of((128, 2048), F32), shape_of((128, 2048))],
         scratch_shapes=[pltpu.VMEM((PAIR, 512, 256), F32)],

time: 171 us -> 170 us (level)
  no operation moved by 1% of the time
where the time goes in v5:
time: 170 us; the launch traced here: 169 us
  blocking collectives  113 us (66%)
  starting transfers between devices  28.3 us (17%)
  Pallas kernels  15.4 us (9%)
  waiting for transfers between devices  9 us (5%)
  local copies, waits for them, and re-layouts  2.54 us (1%)
    all_to_all x1, blocking collectives, per_device(): lax.all_to_all(parts, 'z', 0, 0, tiled=True, axis_index_groups=FAR_GROUPS)  35.9 us
    all_gather x1, blocking collectives, per_device(): lon = lax.all_gather(lon, 'z', axis=0, tiled=True)  32 us
    all_gather x1, blocking collectives, per_device(): lax.all_gather(forcing, 'z', axis=0, tiled=True, axis_index_groups=BACKWARD)  28.4 us
    all_to_all x1, blocking collectives, per_device(): back = lax.all_to_all(back, ('pair', 'chip'), 0, 0, tiled=True)  16.2 us
    ppermute x1, starting transfers between devices, per_device(): got = lax.ppermute(give, 'core', SWAP)  10.5 us
    all_to_all x1, starting transfers between devices, per_device(): lax.all_to_all(own_control, ('pair', 'chip', 'core'), 0, 0, tiled=True)  10.5 us
    ppermute x1, waiting for transfers between devices, per_device(): got = lax.ppermute(give, 'z', [(z, z ^ 1) for z in range(RING)])  4.97 us
    pallas_call x1, Pallas kernels, per_device(): pl.pallas_call(columns_kernel, grid=(4,), in_specs=[pl.BlockSpec((128, 30...  4.78 us
  transfers between devices with their start and end apart: 5, of which 3 were waited for; matrix products, arithmetic and copies ran while one was open for 0% of the time, Pallas kernels for 5%

profile of v5, /device:TPU:1, one launch (start us, length us, event | category | flops | bytes accessed | tf_op | source)
XLA Modules:
  0.0 169.4 jit_solution(11123147928692952109)
XLA Ops:
  0.6 0.8 convert_element_type.12
  1.5 1.1 broadcast_in_dim.3
  2.6 10.5 %all-to-all-start = ((bf16[32,8,2048]{2,1,0:T(8,128)(2,1)}), bf16[32,8,2048]{2,1,0:T(8,128)(2,1)S(1)}, u32[]{:S(2)}, u32[]{:S(2)}) async-start(bf16[32,8,2048]{2,1,0:T(8,128)(2,1)} %broadcast_in_dim.3), calls=%async_computation | async-start | bytes 2097152 | tf_op jit(solution)/shard_map/all_to_all | solution.py:213
  13.1 2.5 %shard_map.77.before_ref = bf16[2,1536,128]{2,1,0:T(8,128)(2,1)} custom-call(bf16[512,3072]{1,0:T(8,128)(2,1)} %bitcast.26), custom_call_target="tpu_custom_call" | custom-call | tf_op jit(solution)/shard_map/pallas_call | solution.py:184
  15.6 0.0 copy-start.3
  15.6 3.5 %collective-permute-start = (bf16[2,1536,128]{2,1,0:T(8,128)(2,1)}, bf16[2,1536,128]{2,1,0:T(8,128)(2,1)S(1)}, u32[]{:S(2)}, u32[]{:S(2)}) collective-permute-start(bf16[2,1536,128]{2,1,0:T(8,128)(2,1)} %shard_map.77.before_ref), channel_id=1, source_target_pairs={{0,16},{16,0},{1,17},{17,1},{2,18},{18,2},{3,19},{19,3},{4,20},{20... | collective-permute-start | bytes 2359304 | tf_op jit(solution)/shard_map/ppermute | solution.py:210
  19.1 4.8 %shard_map.78 = (bf16[4,1536,128]{2,1,0:T(8,128)(2,1)}, bf16[2,1536,128]{2,1,0:T(8,128)(2,1)}, bf16[96,256]{1,0:T(8,128)(2,1)}) custom-call(bf16[512,3072]{1,0:T(8,128)(2,1)} %bitcast.27, bf16[96,256]{1,0:T(8,128)(2,1)} %lon_ref.1, bf16[2,1536,128]{2,1,0:T(8,128)(2,1)} %shard_map.77.before_ref), custom_call_target="tpu_custom_call" | custom-call | tf_op jit(solution)/shard_map/pallas_call | solution.py:193
  23.9 1.9 %collective-permute-start.1 = (bf16[2,1536,128]{2,1,0:T(8,128)(2,1)}, bf16[2,1536,128]{2,1,0:T(8,128)(2,1)S(1)}, u32[]{:S(2)}, u32[]{:S(2)}) collective-permute-start(bf16[2,1536,128]{2,1,0:T(8,128)(2,1)} %get-tuple-element.12), channel_id=1, source_target_pairs={{0,16},{16,0},{1,17},{17,1},{2,18},{18,2},{3,19},{19,3},{4,20},{20... | collective-permute-start | bytes 2359304 | tf_op jit(solution)/shard_map/ppermute | solution.py:211
  25.8 32.0 %all_gather.6 = bf16[1536,256]{1,0:T(8,128)(2,1)S(1)} all-gather(bf16[96,256]{1,0:T(8,128)(2,1)} %get-tuple-element.13), channel_id=1, replica_groups=mesh['z'=16,'pair'=2,'chip'=8,'core'=2] {'z'}, dimensions={0}, use_global_device_ids=true | all-gather | bytes 835584 | tf_op jit(solution)/shard_map/all_gather | solution.py:212
  57.8 0.0 collective-permute-done.first_ref
  57.8 2.5 %collective-permute-done.1.second_ref = bf16[2,1536,128]{2,1,0:T(8,128)(2,1)S(1)} collective-permute-done((bf16[2,1536,128]{2,1,0:T(8,128)(2,1)}, bf16[2,1536,128]{2,1,0:T(8,128)(2,1)S(1)}, u32[]{:S(2)}, u32[]{:S(2)}) %collective-permute-start.1) | collective-permute-done | bytes 786464 | tf_op jit(solution)/shard_map/ppermute | solution.py:211
  60.3 0.0 all-to-all-done
  60.3 0.0 copy-done.3
  60.4 0.0 copy-start
  60.4 1.4 copy-done
  61.8 1.9 %shard_map.79 = (bf16[8,96,256]{2,1,0:T(8,128)(2,1)S(1)}, bf16[2,512,256]{2,1,0:T(8,128)(2,1)S(1)}) custom-call(bf16[4,1536,128]{2,1,0:T(8,128)(2,1)S(1)} %copy-done, bf16[2,1536,128]{2,1,0:T(8,128)(2,1)S(1)} %collective-permute-done.first_ref, bf16[2,1536,128]{2,1,0:T(8,128)(2,1)S(1)} %collective-permute-done.1.second_ref, bf16[256,2048]{1,0:T(8,128)(2,1)S(1)} %bitcast.19, ...), custom_call_target="tpu_custom_call" | custom-call | tf_op jit(solution)/shard_map/pallas_call | solution.py:221
  63.7 1.9 %collective-permute-start.2 = (bf16[8,96,256]{2,1,0:T(8,128)(2,1)S(1)}, bf16[8,96,256]{2,1,0:T(8,128)(2,1)S(1)}, u32[]{:S(2)}, u32[]{:S(2)}) collective-permute-start(bf16[8,96,256]{2,1,0:T(8,128)(2,1)S(1)} %get-tuple-element.15), channel_id=1, source_target_pairs={{0,32},{32,0},{64,96},{96,64},{128,160},{160,128},{192,224},{224,1... | collective-permute-start | bytes 1179656 | tf_op jit(solution)/shard_map/ppermute | solution.py:230
  65.6 0.0 copy-start.4
  65.6 0.0 copy-start.5
  65.6 1.6 shard_map.80.keep_ref
  67.2 0.0 copy-start.1
  67.2 5.0 %collective-permute-done.2.got_ref = bf16[8,96,256]{2,1,0:T(8,128)(2,1)S(1)} collective-permute-done((bf16[8,96,256]{2,1,0:T(8,128)(2,1)S(1)}, bf16[8,96,256]{2,1,0:T(8,128)(2,1)S(1)}, u32[]{:S(2)}, u32[]{:S(2)}) %collective-permute-start.2) | collective-permute-done | bytes 393248 | tf_op jit(solution)/shard_map/ppermute | solution.py:230
  72.2 0.1 shard_map.81
  72.3 35.9 %all_to_all.24.refs_0_ = bf16[8,96,256]{2,1,0:T(8,128)(2,1)S(1)} all-to-all(bf16[8,96,256]{2,1,0:T(8,128)(2,1)S(1)} %shard_map.81), channel_id=1, replica_groups={{0,256,128,384,64,320,192,448},{32,288,160,416,96,352,224,480},{1,257,1..., dimensions={0} | all-to-all | bytes 786432 | tf_op jit(solution)/shard_map/all_to_all | solution.py:241
  108.1 0.0 copy-done.4
  108.1 0.0 copy-done.5
  108.1 0.8 shard_map.82
  108.9 28.4 %all_gather.7 = bf16[1536,256]{1,0:T(8,128)(2,1)S(1)} all-gather(bf16[96,256]{1,0:T(8,128)(2,1)S(1)} %get-tuple-element.17), channel_id=1, replica_groups={{480,448,416,384,352,320,288,256,224,192,160,128,96,64,32,0},{481,449,4..., dimensions={0}, use_global_device_ids=true | all-gather | bytes 835584 | tf_op jit(solution)/shard_map/all_gather | solution.py:247
  137.4 0.0 copy-done.1
  137.4 0.0 copy-start.2
  137.4 3.0 %shard_map.83 = (f32[128,2048]{1,0:T(8,128)S(1)}, bf16[128,2048]{1,0:T(8,128)(2,1)S(1)}) custom-call(bf16[4,1536,128]{2,1,0:T(8,128)(2,1)S(1)} %copy-done.1, bf16[2,1536,128]{2,1,0:T(8,128)(2,1)S(1)} %collective-permute-done.first_ref, bf16[2,1536,128]{2,1,0:T(8,128)(2,1)S(1)} %collective-permute-done.1.second_ref, bf16[8,2,96,256]{3,2,1,0:T(8,128)(2,1)S(1)} %bitcast.20, ...), custom_call_target="tpu_custom_call" | custom-call | tf_op jit(solution)/shard_map/pallas_call | solution.py:251
  140.4 10.5 %collective-permute-start.3 = (bf16[128,2048]{1,0:T(8,128)(2,1)S(1)}, bf16[128,2048]{1,0:T(8,128)(2,1)S(1)}, u32[]{:S(2)}, u32[]{:S(2)}) collective-permute-start(bf16[128,2048]{1,0:T(8,128)(2,1)S(1)} %get-tuple-element.19), channel_id=1, source_target_pairs={{0,1},{1,0},{2,3},{3,2},{4,5},{5,4},{6,7},{7,6},{8,9},{9,8},{10,11... | collective-permute-start | bytes 1572872 | tf_op jit(solution)/shard_map/ppermute | solution.py:261
  150.9 1.5 collective-permute-done.3.got_ref
  152.4 0.1 shard_map.84
  152.5 16.2 %all_to_all.25 = bf16[16,8,2048]{2,1,0:T(8,128)(2,1)S(1)} all-to-all(bf16[16,8,2048]{2,1,0:T(8,128)(2,1)S(1)} %bitcast.22), channel_id=1, replica_groups=mesh['z'=16,'pair'=2,'chip'=8,'core'=2] {'pair','chip'}, dimensions={0} | all-to-all | bytes 1048576 | tf_op jit(solution)/shard_map/all_to_all | solution.py:263
  168.7 0.0 copy-done.2
  168.7 0.7 shard_map.85
Async XLA Ops:
  2.6 57.8 %all-to-all-start = ((bf16[32,8,2048]{2,1,0:T(8,128)(2,1)}), bf16[32,8,2048]{2,1,0:T(8,128)(2,1)S(1)}, u32[]{:S(2)}, u32[]{:S(2)}) async-start(bf16[32,8,2048]{2,1,0:T(8,128)(2,1)} %broadcast_in_dim.3), calls=%async_computation | async-start | bytes 2097152 | tf_op jit(solution)/shard_map/all_to_all | solution.py:213
  15.6 44.8 %copy-start.3 = (bf16[64,128]{1,0:T(8,128)(2,1)S(1)}, bf16[64,128]{1,0:T(8,128)(2,1)}, u32[]{:S(2)}) copy-start(bf16[64,128]{1,0:T(8,128)(2,1)} %lat_ref.3) | copy-start | bytes 49156
  15.6 42.3 %collective-permute-start = (bf16[2,1536,128]{2,1,0:T(8,128)(2,1)}, bf16[2,1536,128]{2,1,0:T(8,128)(2,1)S(1)}, u32[]{:S(2)}, u32[]{:S(2)}) collective-permute-start(bf16[2,1536,128]{2,1,0:T(8,128)(2,1)} %shard_map.77.before_ref), channel_id=1, source_target_pairs={{0,16},{16,0},{1,17},{17,1},{2,18},{18,2},{3,19},{19,3},{4,20},{20... | collective-permute-start | bytes 2359304 | tf_op jit(solution)/shard_map/ppermute | solution.py:210
  23.9 36.5 %collective-permute-start.1 = (bf16[2,1536,128]{2,1,0:T(8,128)(2,1)}, bf16[2,1536,128]{2,1,0:T(8,128)(2,1)S(1)}, u32[]{:S(2)}, u32[]{:S(2)}) collective-permute-start(bf16[2,1536,128]{2,1,0:T(8,128)(2,1)} %get-tuple-element.12), channel_id=1, source_target_pairs={{0,16},{16,0},{1,17},{17,1},{2,18},{18,2},{3,19},{19,3},{4,20},{20... | collective-permute-start | bytes 2359304 | tf_op jit(solution)/shard_map/ppermute | solution.py:211
  60.4 1.4 copy-start
  63.7 8.5 %collective-permute-start.2 = (bf16[8,96,256]{2,1,0:T(8,128)(2,1)S(1)}, bf16[8,96,256]{2,1,0:T(8,128)(2,1)S(1)}, u32[]{:S(2)}, u32[]{:S(2)}) collective-permute-start(bf16[8,96,256]{2,1,0:T(8,128)(2,1)S(1)} %get-tuple-element.15), channel_id=1, source_target_pairs={{0,32},{32,0},{64,96},{96,64},{128,160},{160,128},{192,224},{224,1... | collective-permute-start | bytes 1179656 | tf_op jit(solution)/shard_map/ppermute | solution.py:230
  65.6 42.5 %copy-start.4 = (bf16[2,2,64,96]{3,2,1,0:T(8,128)(2,1)S(1)}, bf16[2,2,64,96]{3,2,1,0:T(8,128)(2,1)}, u32[]{:S(2)}) copy-start(bf16[2,2,64,96]{3,2,1,0:T(8,128)(2,1)} %param.10) | copy-start | bytes 147460
  65.6 42.5 %copy-start.5 = (bf16[2,2,64,96]{3,2,1,0:T(8,128)(2,1)S(1)}, bf16[2,2,64,96]{3,2,1,0:T(8,128)(2,1)}, u32[]{:S(2)}) copy-start(bf16[2,2,64,96]{3,2,1,0:T(8,128)(2,1)} %param.11) | copy-start | bytes 147460
  67.2 70.2 %copy-start.1 = (bf16[4,1536,128]{2,1,0:T(8,128)(2,1)S(1)}, bf16[4,1536,128]{2,1,0:T(8,128)(2,1)}, u32[]{:S(2)}) copy-start(bf16[4,1536,128]{2,1,0:T(8,128)(2,1)} %get-tuple-element.11.own_ref) | copy-start | bytes 4718596
  137.4 31.3 %copy-start.2 = (f32[2,2,2,8,256]{4,3,2,1,0:T(8,128)S(1)}, f32[2,2,2,8,256]{4,3,2,1,0:T(8,128)}, u32[]{:S(2)}) copy-start(f32[2,2,2,8,256]{4,3,2,1,0:T(8,128)} %param.7) | copy-start | bytes 196612
  140.4 12.0 %collective-permute-start.3 = (bf16[128,2048]{1,0:T(8,128)(2,1)S(1)}, bf16[128,2048]{1,0:T(8,128)(2,1)S(1)}, u32[]{:S(2)}, u32[]{:S(2)}) collective-permute-start(bf16[128,2048]{1,0:T(8,128)(2,1)S(1)} %get-tuple-element.19), channel_id=1, source_target_pairs={{0,1},{1,0},{2,3},{3,2},{4,5},{5,4},{6,7},{7,6},{8,9},{9,8},{10,11... | collective-permute-start | bytes 1572872 | tf_op jit(solution)/shard_map/ppermute | solution.py:261
